TPU v7x, 32 devices: a whole 2x2x4 slice. The times are simulated.
32 devices in a mesh: rep: 4 (over y, core), sp: 8 (over z, x).
Axes of the slice: x: 2, y: 2, z: 4, core: 2. Of those that a mesh axis runs over, the one named last changes fastest.
Arguments:
- film_start: float32 [4, 128, 128], P('rep', 'sp'), may hold values from 0.2 to 2
- evaporation: float32 [4, 128, 128], P('rep', 'sp'), may hold values from 0.05 to 0.5
- contact_mask: int32 [4, 128, 128], P('rep', 'sp'), may hold values 0 or 1
- first_classes: int32 [4, 128, 1], P('rep'), may hold values from 0 to 3
- second_classes: int32 [4, 128, 1], P('rep', 'sp'), may hold values from 0 to 3
- span_inverses: float32 [4, 128, 128], replicated, may hold values from -0.4 to 1
- conv_weight: bfloat16 [3, 3, 4, 64], replicated, may hold values from -0.5 to 0.5
- mixing_weight: bfloat16 [64, 64], replicated, may hold values from -0.75 to 0.75
- flux_weight: bfloat16 [64], replicated, may hold values from -0.75 to 0.75
- film_cotangent: float32 [4, 128, 128], P('rep', 'sp'), may hold values from -6 to 6
Outputs:
- final_film: float32 [4, 128, 128], P('rep', 'sp')
- film_grad: float32 [4, 128, 128], P('rep', 'sp')
- conv_grad: float32 [3, 3, 4, 64], replicated
- mixing_grad: float32 [64, 64], replicated
- flux_grad: float32 [64], replicated
All inputs are finite; a program needn't handle non-finite values. No bound on the sum of `contact_mask` on one device may be relied on, other than what follows from the above.
Results may differ from a plain program's by a relative error of at most 0.019.
Values may be sent and summed in bfloat16 or wider, within the bound.
No kernel may reach another device: no remote copies, remote signals or barrier semaphores. Data moves between devices by JAX's collectives and lax.ppermute only.
A program may use at most 128 MiB of HBM per device.

v0:
```python
from functools import partial
import math

import jax
import jax.numpy as jnp
from jax import lax
from jax.experimental import pallas as pl
from jax.experimental.pallas import tpu as pltpu
from jax.sharding import PartitionSpec as P

STEPS = 1


time_step = 0.5


def extended(array, sides, width):
    for axis, dim in sides:
        size, length = (lax.axis_size(axis), array.shape[dim])
        up = [(i, (i + 1) % size) for i in range(size - 1)]
        down = [(j, i) for i, j in up]
        last = lax.slice_in_dim(array, length - width, length, axis=dim)
        first = lax.slice_in_dim(array, 0, width, axis=dim)
        before = lax.ppermute(last, axis, up)
        after = lax.ppermute(first, axis, down)
        array = jnp.concatenate([before, array, after], axis=dim)
    return array


def select_product(tile_rows, matrix, hits, current):
    product = jnp.dot(tile_rows, matrix, precision=lax.Precision.HIGHEST)
    return jnp.where(hits[:, None], product, current)


def keep_same(current):
    return current


def apply_spans(vectors, classes, inverses, transpose):
    count = vectors.shape[0]
    tile_size = math.gcd(128, count)
    line_order = jnp.argsort(classes, stable=True)
    ordered = jnp.take(vectors, line_order, axis=0)
    ordered_cls = jnp.take(classes, line_order)
    results = []
    for start in range(0, count, tile_size):
        tile_rows = ordered[start : start + tile_size]
        tile_cls = ordered_cls[start : start + tile_size]
        result = jnp.zeros_like(tile_rows)
        for group in range(inverses.shape[0]):
            matrix = inverses[group] if transpose else inverses[group].T
            hits = tile_cls == group
            result = lax.cond(
                jnp.any(hits), partial(select_product, tile_rows, matrix, hits), keep_same, result
            )
        results.append(result)
    joined = jnp.concatenate(results, axis=0)
    return jnp.zeros_like(vectors).at[line_order].set(joined)


def solve_lines(lines, classes, inverses, transpose):
    span = inverses.shape[1]
    vectors = lines.reshape(-1, span)
    return apply_spans(vectors, classes.reshape(-1), inverses, transpose).reshape(lines.shape)


def relayout(field):
    moved = lax.all_to_all(field, "sp", split_axis=2, concat_axis=1, tiled=True)
    return jnp.swapaxes(moved, 1, 2)


def split_columns(padded, width):
    count = (padded.shape[-1] - 2) // width
    return jnp.stack(
        [padded[..., number * width : number * width + width + 2] for number in range(count)]
    )


def join_blocks(blocks):
    moved = jnp.moveaxis(blocks, 0, -2)
    return moved.reshape(moved.shape[:-2] + (moved.shape[-2] * moved.shape[-1],))


def cut_blocks(field, width):
    shape = field.shape
    reshaped = field.reshape(shape[:-1] + (shape[-1] // width, width))
    return jnp.moveaxis(reshaped, -2, 0)


def join_padded(blocks):
    middle = jnp.moveaxis(blocks[..., 1:-1], 0, -2)
    left = jnp.moveaxis(blocks[..., 0], 0, -1)
    right = jnp.moveaxis(blocks[..., -1], 0, -1)
    middle = middle.at[..., :-1, -1].add(left[..., 1:])
    middle = middle.at[..., 1:, 0].add(right[..., :-1])
    return middle.reshape(middle.shape[:-2] + (middle.shape[-2] * middle.shape[-1],))


def tap_stack(piece):
    rows = piece.shape[2] - 2
    cols = piece.shape[3] - 2
    return jnp.concatenate(
        [
            piece[:, :, row_tap : row_tap + rows, col_tap : col_tap + cols]
            for row_tap in range(3)
            for col_tap in range(3)
        ],
        axis=0,
    )


def closure_forward(piece, conv_w, mixing_w, flux_w):
    stacked = tap_stack(piece)
    conv_matrix = conv_w.reshape(-1, conv_w.shape[-1])
    first_tanh = jnp.tanh(
        jnp.einsum("ko,krxy->orxy", conv_matrix, stacked, preferred_element_type=jnp.float32)
    )
    first_act = first_tanh.astype(jnp.bfloat16)
    second_tanh = jnp.tanh(
        jnp.einsum("op,orxy->prxy", mixing_w, first_act, preferred_element_type=jnp.float32)
    )
    second_act = second_tanh.astype(jnp.bfloat16)
    flux = jnp.einsum("p,prxy->rxy", flux_w, second_act, preferred_element_type=jnp.float32)
    return (flux, first_tanh, first_act, second_tanh, second_act, stacked)


def closure_backward(piece, flux_cot, conv_w, mixing_w, flux_w):
    rows = piece.shape[2] - 2
    cols = piece.shape[3] - 2
    channels = piece.shape[0]
    flux, first_tanh, first_act, second_tanh, second_act, stacked = closure_forward(
        piece, conv_w, mixing_w, flux_w
    )
    flux_part = jnp.einsum("prxy,rxy->p", second_act, flux_cot, preferred_element_type=jnp.float32)
    second_cot = (flux_w.astype(jnp.float32)[:, None, None, None] * flux_cot[None]).astype(
        jnp.bfloat16
    )
    pre_second_cot = second_cot * (1.0 - second_tanh * second_tanh)
    mixing_part = jnp.einsum(
        "orxy,prxy->op", first_act, pre_second_cot, preferred_element_type=jnp.float32
    )
    first_cot = jnp.einsum(
        "op,prxy->orxy", mixing_w, pre_second_cot, preferred_element_type=jnp.float32
    ).astype(jnp.bfloat16)
    pre_first_cot = first_cot * (1.0 - first_tanh * first_tanh)
    conv_part = jnp.einsum(
        "orxy,krxy->ko", pre_first_cot, stacked, preferred_element_type=jnp.float32
    ).reshape(conv_w.shape)
    conv_matrix = conv_w.reshape(-1, conv_w.shape[-1])
    tap_cots = jnp.einsum(
        "ko,orxy->krxy", conv_matrix, pre_first_cot, preferred_element_type=jnp.float32
    )
    piece_cot = jnp.zeros(piece.shape, jnp.float32)
    for row_tap in range(3):
        for col_tap in range(3):
            number = row_tap * 3 + col_tap
            term = tap_cots[number * channels : (number + 1) * channels]
            piece_cot = piece_cot.at[:, :, row_tap : row_tap + rows, col_tap : col_tap + cols].add(
                term
            )
    edges = jnp.stack([pre_first_cot[:, :, 0], pre_first_cot[:, :, -1]], axis=2)
    return (piece_cot, conv_part, mixing_part, flux_part, edges)


def rim_terms(neighbour, conv_w, row_tap, cols):
    padded = jnp.pad(neighbour, ((0, 0), (0, 0), (1, 1)))
    total = None
    for col_tap in range(3):
        term = jnp.einsum(
            "co,ory->cry",
            conv_w[row_tap, col_tap],
            padded[:, :, 2 - col_tap : 2 - col_tap + cols],
            preferred_element_type=jnp.float32,
        )
        total = term if total is None else total + term
    return total


def by_slabs(
    film_start,
    evaporation,
    contact_mask,
    first_classes,
    second_classes,
    span_inverses,
    conv_weight,
    mixing_weight,
    flux_weight,
    film_cotangent,
):
    maskf = contact_mask.astype(jnp.float32)
    side = film_start.shape[2]
    side_dev = film_start.shape[1]
    nspan = first_classes.shape[2]
    sp_index = lax.axis_index("sp")
    block_width = min(512, side)

    def first_solve(field, transpose):
        own_first = lax.dynamic_slice(
            first_classes, (0, sp_index * side_dev, 0), (1, side_dev, nspan)
        )
        solved = solve_lines(relayout(field), own_first, span_inverses, transpose)
        return relayout(solved)

    def forward_block(piece):
        return closure_forward(piece, conv_weight, mixing_weight, flux_weight)[0]

    def backward_block(items):
        return closure_backward(items[0], items[1], conv_weight, mixing_weight, flux_weight)

    height = film_start
    step = 0
    features = jnp.stack([height, height * height, maskf, evaporation]).astype(jnp.bfloat16)
    rimmed = extended(features, (("sp", 2),), 1)
    padded = jnp.pad(rimmed, ((0, 0), (0, 0), (0, 0), (1, 1)))
    pieces = split_columns(padded, block_width)
    flux = join_blocks(lax.map(forward_block, pieces))
    source_side = height + time_step * (flux - maskf * evaporation)
    across = first_solve(source_side, False)
    saved = [(height, pieces)]
    height = solve_lines(across, second_classes, span_inverses, False)
    final_film = height
    grad = film_cotangent
    conv_total = jnp.zeros(conv_weight.shape, jnp.float32)
    mixing_total = jnp.zeros(mixing_weight.shape, jnp.float32)
    flux_total = jnp.zeros(flux_weight.shape, jnp.float32)
    for step in reversed(range(STEPS)):
        height, pieces = saved[step]
        back = solve_lines(grad, second_classes, span_inverses, True)
        source_grad = first_solve(back, True)
        flux_cot = cut_blocks(time_step * source_grad, block_width)
        piece_cots, conv_parts, mixing_parts, flux_parts, edges = lax.map(
            backward_block, (pieces, flux_cot)
        )
        conv_total = jnp.sum(conv_parts, axis=0)
        mixing_total = jnp.sum(mixing_parts, axis=0)
        flux_total = jnp.sum(flux_parts, axis=0)
        whole = join_padded(piece_cots)
        inner = whole[:, :, 1:-1]
        rims = extended(join_blocks(edges).astype(jnp.bfloat16), (("sp", 2),), 1).astype(
            jnp.float32
        )
        inner = inner.at[:, :, 0].add(rim_terms(rims[:, :, 0], conv_weight, 2, side))
        inner = inner.at[:, :, -1].add(rim_terms(rims[:, :, 3], conv_weight, 0, side))
        feature_cot = inner.astype(jnp.bfloat16)
        grad = source_grad + feature_cot[0] + 2.0 * height * feature_cot[1]
    conv_sum, mixing_sum, flux_sum = lax.psum((conv_total, mixing_total, flux_total), ("rep", "sp"))
    scale = 1.0 / math.sqrt(lax.axis_size("rep") * film_start.shape[0] * side * side)
    return (final_film, grad, conv_sum * scale, mixing_sum * scale, flux_sum * scale)


NEAR_CHUNK = 32
FAR_CHUNK = 32


def swap(value, axis, bit):
    size = lax.axis_size(axis)
    return lax.ppermute(value, axis, [(i, i ^ bit) for i in range(size)])


def dot(left, right):
    return jnp.dot(left, right, preferred_element_type=jnp.float32)


def dot_lanes(left, right):
    return lax.dot_general(
        left, right, (((1,), (1,)), ((), ())), preferred_element_type=jnp.float32
    )


def halves(value):
    high = value.astype(jnp.bfloat16)
    return high, (value - high.astype(jnp.float32)).astype(jnp.bfloat16)


def prepare_kernel(
    inv_h, conv_h, mixing_h, flux_h, first_h,
    rows, lanes, conv_l, taps_l, mixing, mix_t, flux_col, first_row,
    inv, conv, flux_w, conv_s, sems,
):
    copies = [
        pltpu.make_async_copy(source, target, sems.at[number])
        for number, (source, target) in enumerate(
            ((inv_h, inv), (conv_h, conv), (mixing_h, mixing), (flux_h, flux_w), (first_h, first_row))
        )
    ]
    for copy in copies:
        copy.start()
    for copy in copies:
        copy.wait()
    groups, span, _ = inv.shape
    for group in range(groups):
        matrix = inv[group]
        for number, part in enumerate(halves(matrix) + halves(matrix.T)):
            at = group * span
            rows[number, at : at + span, :] = part
            lanes[number, :, at : at + span] = part
    conv_s[...] = jnp.zeros_like(conv_s)
    hid = conv.shape[3]
    channels = conv.shape[2]
    for row_tap in range(3):
        for col_tap in range(3):
            at = row_tap * 16 + col_tap * channels
            conv_s[at : at + channels, :] = conv[row_tap, col_tap].astype(jnp.float32)
    stacked = conv_s[...]
    conv_l[...] = stacked.T.astype(jnp.bfloat16)
    taps_l[...] = jnp.concatenate(
        [stacked[16 * tap : 16 * tap + 16] for tap in (2, 1, 0)], axis=1
    ).astype(jnp.bfloat16)
    mix_t[...] = mixing[...].astype(jnp.float32).T.astype(jnp.bfloat16)
    wide = jnp.broadcast_to(flux_w[...].astype(jnp.float32), (16, hid))
    flux_col[...] = wide.T[:, :1]


def masked_products(left, rows_high, rows_low, classes, groups):
    high, low = halves(left)
    high = jnp.concatenate([jnp.where(classes == g, high, 0) for g in range(groups)], axis=1)
    low = jnp.concatenate([jnp.where(classes == g, low, 0) for g in range(groups)], axis=1)
    return dot(high, rows_high) + dot(low, rows_high) + dot(high, rows_low)


def products_masked(lanes_high, lanes_low, right, classes, groups):
    high, low = halves(right)
    high = jnp.concatenate([jnp.where(classes == g, high, 0) for g in range(groups)], axis=0)
    low = jnp.concatenate([jnp.where(classes == g, low, 0) for g in range(groups)], axis=0)
    return dot(lanes_high, high) + dot(lanes_high, low) + dot(lanes_low, high)


def unpack(slabs, first_place, place, film_s, rate_s, cot_s, class_s, offset):
    count = len(slabs)
    own_rows = (slabs[0].shape[0] - 8) // 3
    columns = jnp.concatenate([slab[3 * own_rows : 3 * own_rows + 1] for slab in slabs], axis=0).T
    for number, slab in enumerate(slabs):
        at = (first_place ^ number) * own_rows
        whole = pl.ds(pl.multiple_of(at, own_rows), own_rows)
        local = pl.ds(pl.multiple_of(at - offset, own_rows), own_rows)
        film_s[whole, :] = slab[:own_rows]
        rate_s[whole, :] = slab[own_rows : 2 * own_rows]
        cot_s[local, :] = slab[2 * own_rows : 3 * own_rows]
        class_s[local, :] = jnp.broadcast_to(
            columns[:own_rows, number : number + 1], (own_rows, slab.shape[1])
        )


def write_features(height, coded, feat_s):
    rows, side = height.shape
    lane = lax.broadcasted_iota(jnp.int32, (rows, side), 1)
    maskf = jnp.where(coded < 0, 1.0, 0.0)
    feat_s[...] = jnp.zeros_like(feat_s)
    for number, field in enumerate((height, height * height, maskf, jnp.abs(coded))):
        field = field.astype(jnp.bfloat16).astype(jnp.float32)
        before = jnp.where(lane == 0, 0.0, pltpu.roll(field, 1, 1))
        after = jnp.where(lane == side - 1, 0.0, pltpu.roll(field, side - 1, 1))
        for tap, moved in enumerate((before, field, after)):
            feat_s[pl.ds(16 + tap * 4 + number, rows, stride=16), :] = moved


def forward_rows(featb, feat_row, row, count, conv_l, mix_t, weights, act1_s, act2_s, slope1_s, slope2_s, flux_s):
    hid, side = conv_l.shape[0], flux_s.shape[1]
    stacked = jnp.concatenate(
        [featb[pl.ds(pl.multiple_of((feat_row + k) * 16, 16), 48), :] for k in range(count)], axis=1
    )
    first_tanh = jnp.tanh(dot(conv_l[...], stacked))
    first_act = first_tanh.astype(jnp.bfloat16)
    second_tanh = jnp.tanh(dot(mix_t[...], first_act))
    second_act = second_tanh.astype(jnp.bfloat16)
    flux = jnp.sum(second_act.astype(jnp.float32) * weights, axis=0, keepdims=True)
    first_slope = (1.0 - first_tanh * first_tanh).astype(jnp.bfloat16)
    second_slope = (1.0 - second_tanh * second_tanh).astype(jnp.bfloat16)
    for k in range(count):
        at = pl.ds(pl.multiple_of((row + k) * hid, hid), hid)
        lanes = slice(k * side, (k + 1) * side)
        act1_s[at, :] = first_act[:, lanes]
        act2_s[at, :] = second_act[:, lanes]
        slope1_s[at, :] = first_slope[:, lanes]
        slope2_s[at, :] = second_slope[:, lanes]
        flux_s[pl.ds(row + k, 1), :] = flux[:, lanes]


def near_kernel(
    near, rows, conv_l, mix_t, flux_col,
    film_s, rate_s, back_s, featb, act1_s, act2_s, slope1_s, slope2_s, flux_s, class_own,
    cot_s, class_s, feat_s, local_s,
):
    place = lax.axis_index("sp")
    slabs = near.shape[0]
    half, side = cot_s.shape
    groups = rows.shape[1] // side
    base = pl.multiple_of((place // slabs) * half, half)
    unpack([near[n] for n in range(slabs)], place, place, film_s, rate_s, cot_s, class_s, base)
    mine = pl.ds(base, half)
    write_features(film_s[mine, :], rate_s[mine, :], feat_s)
    local_s[...] = feat_s[...].astype(jnp.bfloat16)
    featb[pl.ds(pl.multiple_of((base + 1) * 16, 16), half * 16), :] = local_s[16 : (half + 1) * 16, :]
    class_own[...] = class_s[pl.ds(pl.multiple_of(place * class_own.shape[0] - base, 8), class_own.shape[0]), :]
    weights = flux_col[...]
    for start in range(0, half, NEAR_CHUNK):
        forward_rows(
            local_s, start, base + start, NEAR_CHUNK, conv_l, mix_t, weights,
            act1_s, act2_s, slope1_s, slope2_s, flux_s,
        )
    back_s[mine, :] = masked_products(cot_s[...], rows[0], rows[1], class_s[...], groups)


def far_kernel(
    scale, far, first_cls, rows, lanes, conv_l, mixing, mix_t, flux_col,
    film_i, rate_i, back_i, featb_i, act1_i, act2_i, slope1_i, slope2_i, flux_i,
    grads, source, source_grad, height_own, pre_first,
    film_s, rate_s, back_s, featb, act1_s, act2_s, slope1_s, slope2_s, flux_s,
    cot_s, class_s, feat_s, sgrad_s, pre_s,
):
    place = lax.axis_index("sp")
    slabs = far.shape[0]
    half, side = cot_s.shape
    own_rows = source_grad.shape[0]
    hid = mixing.shape[0]
    groups = rows.shape[1] // side
    upper = place // slabs
    base = pl.multiple_of((1 - upper) * half, half)
    unpack([far[n] for n in range(slabs)], place ^ slabs, place, film_s, rate_s, cot_s, class_s, base)
    mine = pl.ds(base, half)
    back_s[mine, :] = masked_products(cot_s[...], rows[0], rows[1], class_s[...], groups)
    sgrad_s[...] = products_masked(lanes[2], lanes[3], back_s[...], first_cls[...], groups)
    write_features(film_s[mine, :], rate_s[mine, :], feat_s)
    featb[pl.ds(pl.multiple_of((base + 1) * 16, 16), half * 16), :] = feat_s[
        16 : (half + 1) * 16, :
    ].astype(jnp.bfloat16)
    featb[0:16, :] = jnp.zeros((16, side), jnp.bfloat16)
    featb[(side + 1) * 16 :, :] = jnp.zeros((16, side), jnp.bfloat16)

    weights = flux_col[...]
    first = (1 - upper) * (half - 1)
    for start, count in ((0, half // 2), (half // 2, half - half // 2 + 1)):
        forward_rows(
            featb, first + start, first + start, count, conv_l, mix_t, weights,
            act1_s, act2_s, slope1_s, slope2_s, flux_s,
        )

    pre_s[0:hid, :] = jnp.zeros((hid, side), jnp.bfloat16)
    pre_s[(side + 1) * hid :, :] = jnp.zeros((hid, side), jnp.bfloat16)
    mixing_sum = conv_sum = flux_sum = None
    chunk = FAR_CHUNK
    for start in range(0, side, chunk):
        def joined(ref):
            return jnp.concatenate([ref[(start + k) * hid : (start + k + 1) * hid, :] for k in range(chunk)], axis=1)

        flux_cot = time_step * jnp.concatenate(
            [sgrad_s[start + k : start + k + 1, :] for k in range(chunk)], axis=1
        )
        second_cot = (weights * flux_cot).astype(jnp.bfloat16)
        pre_second = second_cot * joined(slope2_s)
        first_cot = dot(mixing[...], pre_second).astype(jnp.bfloat16)
        pre_cot = first_cot * joined(slope1_s)
        for k in range(chunk):
            at = (start + k + 1) * hid
            pre_s[at : at + hid, :] = pre_cot[:, k * side : (k + 1) * side]
        stacked = jnp.concatenate(
            [featb[(start + k) * 16 : (start + k + 3) * 16, :] for k in range(chunk)], axis=1
        )
        mixing_part = dot_lanes(joined(act1_s), pre_second)
        conv_part = dot_lanes(stacked, pre_cot)
        product = joined(act2_s).astype(jnp.float32) * flux_cot
        flux_part = sum(product[:, k * side : (k + 1) * side] for k in range(chunk))
        if start == 0:
            mixing_sum, conv_sum, flux_sum = mixing_part, conv_part, flux_part
        else:
            mixing_sum += mixing_part
            conv_sum += conv_part
            flux_sum += flux_part
    flux_rows = jnp.broadcast_to(jnp.sum(flux_sum, axis=1, keepdims=True), (hid, 16)).T
    side_by_side = jnp.concatenate(
        [mixing_sum, jnp.concatenate([conv_sum, flux_rows], axis=0)], axis=1
    )
    grads[...] = side_by_side * scale
    maskf = jnp.where(rate_s[...] < 0, 1.0, 0.0)
    source[...] = film_s[...] + time_step * (flux_s[...] - maskf * jnp.abs(rate_s[...]))
    at = pl.multiple_of(place * own_rows, own_rows)
    source_grad[...] = sgrad_s[pl.ds(at, own_rows), :]
    height_own[...] = film_s[pl.ds(at, own_rows), :]
    pre_first[...] = pre_s[pl.ds(pl.multiple_of(at * hid, hid), (own_rows + 2) * hid), :]


def field_kernel(
    source, source_grad, height, pre_first, first_cls, second_cls, rows, lanes, taps_l,
    final_film, film_grad, feature_s,
):
    place = lax.axis_index("sp")
    own_rows, side = height.shape
    groups = rows.shape[1] // side
    hid = taps_l.shape[1] // 3
    at = pl.multiple_of(place * own_rows, own_rows)
    mine = pl.ds(at, own_rows)
    across = products_masked(lanes[0, mine, :], lanes[1, mine, :], source[...], first_cls[...], groups)
    final_film[0] = masked_products(across, rows[2], rows[3], second_cls[...], groups)

    stacked = jnp.concatenate(
        [pre_first[k * hid : (k + 3) * hid, :] for k in range(own_rows)], axis=1
    )
    taps = dot(taps_l[...], stacked)
    for k in range(own_rows):
        feature_s[k * 16 : k * 16 + 16, :] = taps[:, k * side : (k + 1) * side]
    lane = lax.broadcasted_iota(jnp.int32, (own_rows, side), 1)
    cots = []
    for channel in range(2):
        first, middle, last = (
            feature_s[pl.ds(tap * 4 + channel, own_rows, stride=16), :] for tap in range(3)
        )
        after = jnp.where(lane == side - 1, 0.0, pltpu.roll(first, side - 1, 1))
        before = jnp.where(lane == 0, 0.0, pltpu.roll(last, 1, 1))
        cots.append((after + middle + before).astype(jnp.bfloat16).astype(jnp.float32))
    film_grad[0] = source_grad[...] + cots[0] + 2.0 * height[...] * cots[1]


def finish_kernel(here, there, conv_grad, mixing_grad, flux_grad):
    total = here[...] + there[...]
    hid = mixing_grad.shape[0]
    channels = conv_grad.shape[2]
    mixing_grad[...] = total[:, :hid]
    other = total[:, hid:]
    for row_tap in range(3):
        for col_tap in range(3):
            at = row_tap * 16 + col_tap * channels
            conv_grad[row_tap, col_tap] = other[at : at + channels]
    flux_grad[...] = other[48:49]


def by_replica(
    film_start,
    evaporation,
    contact_mask,
    first_classes,
    second_classes,
    span_inverses,
    conv_weight,
    mixing_weight,
    flux_weight,
    film_cotangent,
):
    f32, bf16 = jnp.float32, jnp.bfloat16
    own_rows, side = film_start.shape[1:]
    groups = span_inverses.shape[0]
    hid = mixing_weight.shape[0]
    sp, rep = lax.axis_size("sp"), lax.axis_size("rep")
    params = pltpu.CompilerParams(vmem_limit_bytes=40 * 2**20)
    shape = jax.ShapeDtypeStruct

    length = 3 * own_rows + 8

    def placed(value, number):
        at = number * own_rows
        rows, lanes = value.shape[1:]
        return jnp.pad(value, ((0, 0), (at, length - at - rows), (0, side - lanes)))

    rate = placed(evaporation, 1)
    near = jnp.where(placed(contact_mask, 1) != 0, -rate, rate)
    near = near + placed(film_start, 0) + placed(film_cotangent, 2)
    near = near + placed(second_classes.reshape(1, 1, own_rows), 3).astype(f32)
    near = lax.optimization_barrier(near)
    weights = (
        span_inverses,
        conv_weight,
        mixing_weight,
        flux_weight.reshape(1, hid),
        first_classes.reshape(1, side),
    )
    prepared = pl.pallas_call(
        prepare_kernel,
        out_shape=[
            shape((4, groups * side, side), bf16),
            shape((4, side, groups * side), bf16),
            shape((hid, 48), bf16),
            shape((16, 3 * hid), bf16),
            shape((hid, hid), bf16),
            shape((hid, hid), bf16),
            shape((hid, 1), f32),
            shape((1, side), jnp.int32),
        ],
        in_specs=[pl.BlockSpec(memory_space=pltpu.HBM)] * len(weights),
        scratch_shapes=[
            pltpu.VMEM(span_inverses.shape, f32),
            pltpu.VMEM(conv_weight.shape, bf16),
            pltpu.VMEM((1, hid), bf16),
            pltpu.VMEM((48, hid), f32),
            pltpu.SemaphoreType.DMA((len(weights),)),
        ],
        compiler_params=params,
    )(*(pltpu.with_memory_space_constraint(weight, pltpu.HBM) for weight in weights))
    far = None
    bit = 1
    while bit < sp:
        if far is not None:
            near = jnp.concatenate([near, far], axis=0)
            if bit == 2:
                near, prepared = lax.optimization_barrier((near, prepared))
        far = swap(near, "sp", bit)
        bit *= 2

    rows, lanes, conv_l, taps_l, mixing, mix_t, flux_col, first_cls = prepared
    scale = 1.0 / math.sqrt(rep * side * side)
    half = side // 2
    kept = [
        shape((side, side), f32),
        shape((side, side), f32),
        shape((side, side), f32),
        shape(((side + 2) * 16, side), bf16),
        shape((side * hid, side), bf16),
        shape((side * hid, side), bf16),
        shape((side * hid, side), bf16),
        shape((side * hid, side), bf16),
        shape((side, side), f32),
    ]
    *state, second_cls = pl.pallas_call(
        near_kernel,
        out_shape=kept + [shape((own_rows, side), f32)],
        scratch_shapes=[
            pltpu.VMEM((half, side), f32),
            pltpu.VMEM((half, side), f32),
            pltpu.VMEM(((half + 2) * 16, side), f32),
            pltpu.VMEM(((half + 2) * 16, side), bf16),
        ],
        compiler_params=params,
    )(near, rows, conv_l, mix_t, flux_col)
    grads, source, source_grad, height, pre_first, *_ = pl.pallas_call(
        partial(far_kernel, scale),
        out_shape=[
            shape((hid, 2 * hid), f32),
            shape((side, side), f32),
            shape((own_rows, side), f32),
            shape((own_rows, side), f32),
            shape(((own_rows + 2) * hid, side), bf16),
        ]
        + kept,
        input_output_aliases={8 + number: 5 + number for number in range(len(kept))},
        scratch_shapes=[
            pltpu.VMEM((half, side), f32),
            pltpu.VMEM((half, side), f32),
            pltpu.VMEM(((half + 2) * 16, side), f32),
            pltpu.VMEM((side, side), f32),
            pltpu.VMEM(((side + 2) * hid, side), bf16),
        ],
        compiler_params=params,
    )(far, first_cls, rows, lanes, conv_l, mixing, mix_t, flux_col, *state)

    final_film, film_grad = pl.pallas_call(
        field_kernel,
        out_shape=[shape(film_start.shape, f32), shape(film_start.shape, f32)],
        scratch_shapes=[pltpu.VMEM((own_rows * 16, side), f32)],
        compiler_params=params,
    )(source, source_grad, height, pre_first, first_cls, second_cls, rows, lanes, taps_l)

    there = jnp.zeros_like(grads)
    bit = 1
    while bit < rep:
        if bit > 1:
            grads = grads + there
        there = swap(grads, "rep", bit)
        bit *= 2
    conv_grad, mixing_grad, flux_grad = pl.pallas_call(
        finish_kernel,
        out_shape=[shape(conv_weight.shape, f32), shape((hid, hid), f32), shape((1, hid), f32)],
        compiler_params=params,
    )(grads, there)
    return (final_film, film_grad, conv_grad, mixing_grad, flux_grad.reshape(hid))


def on_device(film_start, *others):
    own_rows, side = film_start.shape[1:]
    nspan = others[2].shape[2]
    conv_weight = others[5]
    sp, rep = lax.axis_size("sp"), lax.axis_size("rep")
    small = (
        film_start.shape[0] == 1
        and nspan == 1
        and side == 128
        and own_rows % 16 == 0
        and sp & (sp - 1) == 0
        and rep & (rep - 1) == 0
        and sp > 1
        and conv_weight.shape[2] == 4
        and conv_weight.shape[3] == 64
    )
    return (by_replica if small else by_slabs)(film_start, *others)


def solution(mesh):
    return jax.shard_map(
        on_device,
        mesh=mesh,
        in_specs=(
            P("rep", "sp", None),
            P("rep", "sp", None),
            P("rep", "sp", None),
            P("rep", None, None),
            P("rep", "sp", None),
            P(),
            P(),
            P(),
            P(),
            P("rep", "sp", None),
        ),
        out_specs=(P("rep", "sp", None), P("rep", "sp", None), P(), P(), P()),
        check_vma=False,
    )
```

profile of v0, /device:TPU:0, one launch (start us, length us, event | category | flops | bytes accessed | tf_op | source)
XLA Modules:
  0.0 27.6 jit_solution(904461544772689404)
XLA Ops:
  0.6 0.8 %fusion.2 = f32[1,56,128]{2,1,0:T(8,128)S(1)} fusion(s32[1,1,16]{2,1,0:T(1,128)} %bitcast.4, f32[1,16,128]{2,1,0:T(8,128)} %param.19, f32[1,16,128]{2,1,0:T(8,128)} %param.10, f32[1,16,128]{2,1,0:T(8,128)} %param.11, s32[1,16,128]{2,1,0:T(8,128)} %param.12), kind=kLoop, calls=%fused_computation.4 | loop fusion | flops 50176 | bytes 61504 | tf_op jit(solution)/shard_map/add | solution.py:557
  1.4 2.9 %collective-permute-start = (f32[1,56,128]{2,1,0:T(8,128)S(1)}, f32[1,56,128]{2,1,0:T(8,128)S(1)}, u32[]{:S(2)}, u32[]{:S(2)}) collective-permute-start(f32[1,56,128]{2,1,0:T(8,128)S(1)} %fusion.2), channel_id=1, source_target_pairs={{0,1},{1,0},{2,3},{3,2},{4,5},{5,4},{6,7},{7,6},{8,9},{9,8},{10,11... | collective-permute-start | bytes 86024 | tf_op jit(solution)/shard_map/ppermute | solution.py:258
  4.3 1.2 %shard_map.137 = (bf16[4,512,128]{2,1,0:T(8,128)(2,1)S(1)}, bf16[4,128,512]{2,1,0:T(8,128)(2,1)S(1)}, bf16[64,48]{1,0:T(8,128)(2,1)S(1)}, bf16[16,192]{1,0:T(8,1...) custom-call(f32[4,128,128]{2,1,0:T(8,128)} %inv_h.1, ...), custom_call_target="tpu_custom_call" | custom-call | tf_op jit(solution)/shard_map/pallas_call | solution.py:566
  5.5 0.6 %collective-permute-done = f32[1,56,128]{2,1,0:T(8,128)S(1)} collective-permute-done((f32[1,56,128]{2,1,0:T(8,128)S(1)}, f32[1,56,128]{2,1,0:T(8,128)S(1)}, u32[]{:S(2)}, u32[]{:S(2)}) %collective-permute-start) | collective-permute-done | bytes 28704 | tf_op jit(solution)/shard_map/ppermute | solution.py:258
  6.2 2.1 %collective-permute-start.1 = (f32[2,56,128]{2,1,0:T(8,128)S(1)}, f32[2,56,128]{2,1,0:T(8,128)S(1)}, u32[]{:S(2)}, u32[]{:S(2)}) collective-permute-start(f32[2,56,128]{2,1,0:T(8,128)S(1)} %pad_maximum_fusion), channel_id=1, source_target_pairs={{0,2},{1,3},{2,0},{3,1},{4,6},{5,7},{6,4},{7,5},{8,10},{9,11},{10,... | collective-permute-start | bytes 172040 | tf_op jit(solution)/shard_map/ppermute | solution.py:258
  8.3 2.1 %collective-permute-done.1 = f32[2,56,128]{2,1,0:T(8,128)S(1)} collective-permute-done((f32[2,56,128]{2,1,0:T(8,128)S(1)}, f32[2,56,128]{2,1,0:T(8,128)S(1)}, u32[]{:S(2)}, u32[]{:S(2)}) %collective-permute-start.1) | collective-permute-done | bytes 57376 | tf_op jit(solution)/shard_map/ppermute | solution.py:258
  10.5 3.0 %collective-permute-start.2 = (f32[4,56,128]{2,1,0:T(8,128)S(1)}, f32[4,56,128]{2,1,0:T(8,128)S(1)}, u32[]{:S(2)}, u32[]{:S(2)}) collective-permute-start(f32[4,56,128]{2,1,0:T(8,128)S(1)} %constant_dynamic-update-slice_fusion.near), channel_id=1, source_target_pairs={{0,4},{1,5},{2,6},{3,7},{4,0},{5,1},{6,2},{7,3},{8,12},{9,13},{10,... | collective-permute-start | bytes 344072 | tf_op jit(solution)/shard_map/ppermute | solution.py:258
  13.5 1.4 %shard_map.138 = (f32[128,128]{1,0:T(8,128)S(1)}, f32[128,128]{1,0:T(8,128)S(1)}, f32[128,128]{1,0:T(8,128)S(1)}, bf16[2080,128]{1,0:T(8,128)(2,1)S(1)}, bf16[81...) custom-call(f32[4,56,128]{2,1,0:T(8,128)S(1)} %constant_dynamic-upda, ...), custom_call_target="tpu_custom_call" | custom-call | tf_op jit(solution)/shard_map/pallas_call | solution.py:612
  14.9 1.4 %collective-permute-done.2.far = f32[4,56,128]{2,1,0:T(8,128)S(1)} collective-permute-done((f32[4,56,128]{2,1,0:T(8,128)S(1)}, f32[4,56,128]{2,1,0:T(8,128)S(1)}, u32[]{:S(2)}, u32[]{:S(2)}) %collective-permute-start.2) | collective-permute-done | bytes 114720 | tf_op jit(solution)/shard_map/ppermute | solution.py:258
  16.3 4.4 %shard_map.139 = (f32[64,128]{1,0:T(8,128)S(1)}, f32[128,128]{1,0:T(8,128)S(1)}, f32[16,128]{1,0:T(8,128)S(1)}, f32[16,128]{1,0:T(8,128)S(1)}, bf16[1152,128]{1,...) custom-call(f32[4,56,128]{2,1,0:T(8,128)S(1)} %collective-permute-do, ...), custom_call_target="tpu_custom_call", output_to_operand_aliasing={{5}: (8, {}), {6}: (9, {}), {7}: (10, {}), {8}: (11, {}), {... | custom-call | tf_op jit(solution)/shard_map/pallas_call | solution.py:623
  20.6 0.1 collective-permute-start.3
  20.7 1.2 %collective-permute-done.3 = f32[64,128]{1,0:T(8,128)S(1)} collective-permute-done((f32[64,128]{1,0:T(8,128)S(1)}, f32[64,128]{1,0:T(8,128)S(1)}, u32[]{:S(2)}, u32[]{:S(2)}) %collective-permute-start.3) | collective-permute-done | bytes 32800 | tf_op jit(solution)/shard_map/ppermute | solution.py:258
  21.9 3.1 %collective-permute-start.4 = (f32[64,128]{1,0:T(8,128)S(1)}, f32[64,128]{1,0:T(8,128)S(1)}, u32[]{:S(2)}, u32[]{:S(2)}) collective-permute-start(f32[64,128]{1,0:T(8,128)S(1)} %add.25.here), channel_id=1, source_target_pairs={{0,16},{8,24},{16,0},{24,8},{1,17},{9,25},{17,1},{25,9},{2,18},{10... | collective-permute-start | bytes 98312 | tf_op jit(solution)/shard_map/ppermute | solution.py:258
  25.0 1.1 %shard_map.140 = (f32[1,16,128]{2,1,0:T(8,128)}, f32[1,16,128]{2,1,0:T(8,128)}) custom-call(f32[128,128]{1,0:T(8,128)S(1)} %get-tuple-element.67.source, f32[16,128]{1,0:T(8,128)S(1)} %get-tuple-element.68.source_grad, f32[16,128]{1,0:T(8,128)S(1)} %get-tuple-element.69.height, bf16[1152,128]{1,0:T(8,128)(2,1)S(1)} %get-tuple-element.70.pre_first, ...), custom_call_target="tpu_custom_call" | custom-call | tf_op jit(solution)/shard_map/pallas_call | solution.py:644
  26.1 0.8 %collective-permute-done.4.there = f32[64,128]{1,0:T(8,128)S(1)} collective-permute-done((f32[64,128]{1,0:T(8,128)S(1)}, f32[64,128]{1,0:T(8,128)S(1)}, u32[]{:S(2)}, u32[]{:S(2)}) %collective-permute-start.4) | collective-permute-done | bytes 32800 | tf_op jit(solution)/shard_map/ppermute | solution.py:258
  26.9 0.7 %shard_map.141 = (f32[3,3,4,64]{3,2,1,0:T(4,128)}, f32[64,64]{1,0:T(8,128)}, f32[1,64]{1,0:T(1,128)}) custom-call(f32[64,128]{1,0:T(8,128)S(1)} %add.25.here, f32[64,128]{1,0:T(8,128)S(1)} %collective-permute-done.4.there), custom_call_target="tpu_custom_call" | custom-call | tf_op jit(solution)/shard_map/pallas_call | solution.py:658
  (4 shorter events, 0.0 us)
Async XLA Ops:
  1.4 4.8 %collective-permute-start = (f32[1,56,128]{2,1,0:T(8,128)S(1)}, f32[1,56,128]{2,1,0:T(8,128)S(1)}, u32[]{:S(2)}, u32[]{:S(2)}) collective-permute-start(f32[1,56,128]{2,1,0:T(8,128)S(1)} %fusion.2), channel_id=1, source_target_pairs={{0,1},{1,0},{2,3},{3,2},{4,5},{5,4},{6,7},{7,6},{8,9},{9,8},{10,11... | collective-permute-start | bytes 86024 | tf_op jit(solution)/shard_map/ppermute | solution.py:258
  6.2 4.3 %collective-permute-start.1 = (f32[2,56,128]{2,1,0:T(8,128)S(1)}, f32[2,56,128]{2,1,0:T(8,128)S(1)}, u32[]{:S(2)}, u32[]{:S(2)}) collective-permute-start(f32[2,56,128]{2,1,0:T(8,128)S(1)} %pad_maximum_fusion), channel_id=1, source_target_pairs={{0,2},{1,3},{2,0},{3,1},{4,6},{5,7},{6,4},{7,5},{8,10},{9,11},{10,... | collective-permute-start | bytes 172040 | tf_op jit(solution)/shard_map/ppermute | solution.py:258
  10.5 5.8 %collective-permute-start.2 = (f32[4,56,128]{2,1,0:T(8,128)S(1)}, f32[4,56,128]{2,1,0:T(8,128)S(1)}, u32[]{:S(2)}, u32[]{:S(2)}) collective-permute-start(f32[4,56,128]{2,1,0:T(8,128)S(1)} %constant_dynamic-update-slice_fusion.near), channel_id=1, source_target_pairs={{0,4},{1,5},{2,6},{3,7},{4,0},{5,1},{6,2},{7,3},{8,12},{9,13},{10,... | collective-permute-start | bytes 344072 | tf_op jit(solution)/shard_map/ppermute | solution.py:258
  20.6 1.3 %collective-permute-start.3 = (f32[64,128]{1,0:T(8,128)S(1)}, f32[64,128]{1,0:T(8,128)S(1)}, u32[]{:S(2)}, u32[]{:S(2)}) collective-permute-start(f32[64,128]{1,0:T(8,128)S(1)} %get-tuple-element.75), channel_id=1, source_target_pairs={{0,8},{8,0},{16,24},{24,16},{1,9},{9,1},{17,25},{25,17},{2,10},{10... | collective-permute-start | bytes 98312 | tf_op jit(solution)/shard_map/ppermute | solution.py:258
  21.9 5.0 %collective-permute-start.4 = (f32[64,128]{1,0:T(8,128)S(1)}, f32[64,128]{1,0:T(8,128)S(1)}, u32[]{:S(2)}, u32[]{:S(2)}) collective-permute-start(f32[64,128]{1,0:T(8,128)S(1)} %add.25.here), channel_id=1, source_target_pairs={{0,16},{8,24},{16,0},{24,8},{1,17},{9,25},{17,1},{25,9},{2,18},{10... | collective-permute-start | bytes 98312 | tf_op jit(solution)/shard_map/ppermute | solution.py:258
where the time goes:
time: 27.8 us; the launch traced here: 27.6 us
  starting transfers between devices  11.2 us (40%)
  Pallas kernels  8.73 us (31%)
  waiting for transfers between devices  6.14 us (22%)
  other arithmetic  0.78 us (3%)
  between operations  0.67 us (2%)
    ppermute x5, starting transfers between devices, swap(): return lax.ppermute(value, axis, [(i, i ^ bit) for i in range(size)])  11.2 us
    ppermute x5, waiting for transfers between devices, swap(): return lax.ppermute(value, axis, [(i, i ^ bit) for i in range(size)])  6.14 us
    pallas_call x1, Pallas kernels, by_replica(): pl.pallas_call(partial(far_kernel, scale), out_shape=[shape((hid, 2 * hid...  4.36 us
    pallas_call x1, Pallas kernels, by_replica(): pl.pallas_call(near_kernel, out_shape=kept + [shape((own_rows, side), f32...  1.38 us
    pallas_call x1, Pallas kernels, by_replica(): pl.pallas_call(prepare_kernel, out_shape=[shape((4, groups * side, side),...  1.19 us
    pallas_call x1, Pallas kernels, by_replica(): pl.pallas_call(field_kernel, out_shape=[shape(film_start.shape, f32), sha...  1.12 us
    add x1, other arithmetic, by_replica(): near = near + placed(second_classes.reshape(1, 1, own_rows), 3).astype(f32)  0.77 us
    pallas_call x1, Pallas kernels, by_replica(): pl.pallas_call(finish_kernel, out_shape=[shape(conv_weight.shape, f32), s...  0.68 us
  transfers between devices with their start and end apart: 5, of which 5 were waited for; matrix products, arithmetic and copies ran while one was open for 0% of the time, Pallas kernels for 13%

commit v1 on v0

--- a/solution.py
+++ b/solution.py
@@ -249,6 +249,8 @@
     return (final_film, grad, conv_sum * scale, mixing_sum * scale, flux_sum * scale)
 
 
+PLANES = 4
+VMEM_VALUES = 2**20
 NEAR_CHUNK = 32
 FAR_CHUNK = 32
 
@@ -271,6 +273,39 @@
 def halves(value):
     high = value.astype(jnp.bfloat16)
     return high, (value - high.astype(jnp.float32)).astype(jnp.bfloat16)
+
+
+def class_bits(groups):
+    return max(1, (groups - 1).bit_length())
+
+
+def pack_kernel(
+    groups, film_h, rate_h, mask_h, class_h, cot_h, packed, film, rate_s, mask_s, class_s, cot_s, sems
+):
+    copies = [
+        pltpu.make_async_copy(source, target, sems.at[number])
+        for number, (source, target) in enumerate(
+            ((film_h, film), (rate_h, rate_s), (mask_h, mask_s), (class_h, class_s), (cot_h, cot_s))
+        )
+    ]
+    for copy in copies:
+        copy.start()
+    for copy in copies:
+        copy.wait()
+    rows, side = film.shape[1:]
+    bits = class_bits(groups)
+    classes = jnp.broadcast_to(class_s[...].astype(jnp.float32), (side, rows)).T.astype(jnp.int32)
+    lane = lax.broadcasted_iota(jnp.int32, (rows, side), 1)
+    bit = jnp.zeros((rows, side), jnp.int32)
+    for number in range(bits):
+        bit = jnp.where(lane // (side // bits) == number, (classes >> number) & 1, bit)
+    high, low = halves(film[0])
+    packed[0, :rows] = jnp.where(bit != 0, -high, high)
+    rate = rate_s[0].astype(jnp.bfloat16)
+    packed[0, rows : 2 * rows] = jnp.where(mask_s[0] != 0, -rate, rate)
+    packed[0, 2 * rows : 3 * rows] = cot_s[0].astype(jnp.bfloat16)
+    if packed.shape[1] > 3 * rows:
+        packed[0, 3 * rows :] = low
 
 
 def prepare_kernel(
@@ -326,20 +361,25 @@
     return dot(lanes_high, high) + dot(lanes_high, low) + dot(lanes_low, high)
 
 
-def unpack(slabs, first_place, place, film_s, rate_s, cot_s, class_s, offset):
-    count = len(slabs)
-    own_rows = (slabs[0].shape[0] - 8) // 3
-    columns = jnp.concatenate([slab[3 * own_rows : 3 * own_rows + 1] for slab in slabs], axis=0).T
+def unpack(slabs, first_place, groups, film_s, rate_s, cot_s, class_s, offset):
+    rows, side = class_s.shape[0] // len(slabs), class_s.shape[1]
+    bits = class_bits(groups)
     for number, slab in enumerate(slabs):
-        at = (first_place ^ number) * own_rows
-        whole = pl.ds(pl.multiple_of(at, own_rows), own_rows)
-        local = pl.ds(pl.multiple_of(at - offset, own_rows), own_rows)
-        film_s[whole, :] = slab[:own_rows]
-        rate_s[whole, :] = slab[own_rows : 2 * own_rows]
-        cot_s[local, :] = slab[2 * own_rows : 3 * own_rows]
-        class_s[local, :] = jnp.broadcast_to(
-            columns[:own_rows, number : number + 1], (own_rows, slab.shape[1])
-        )
+        at = (first_place ^ number) * rows
+        whole = pl.ds(pl.multiple_of(at, rows), rows)
+        local = pl.ds(pl.multiple_of(at - offset, rows), rows)
+        film = slab[:rows].astype(jnp.float32)
+        classes = sum(
+            jnp.where(film[:, bit * (side // bits) : bit * (side // bits) + 1] < 0, 1.0 * 2**bit, 0.0)
+            for bit in range(bits)
+        )
+        class_s[local, :] = jnp.broadcast_to(classes, (rows, side))
+        film = jnp.abs(film)
+        if slab.shape[0] > 3 * rows:
+            film = film + slab[3 * rows :].astype(jnp.float32)
+        film_s[whole, :] = film
+        rate_s[whole, :] = slab[rows : 2 * rows].astype(jnp.float32)
+        cot_s[local, :] = slab[2 * rows : 3 * rows].astype(jnp.float32)
 
 
 def write_features(height, coded, feat_s):
@@ -364,9 +404,9 @@
     first_act = first_tanh.astype(jnp.bfloat16)
     second_tanh = jnp.tanh(dot(mix_t[...], first_act))
     second_act = second_tanh.astype(jnp.bfloat16)
-    flux = jnp.sum(second_act.astype(jnp.float32) * weights, axis=0, keepdims=True)
+    flux = dot(jnp.broadcast_to(weights, (hid, 128)).T[:16].astype(jnp.bfloat16), second_act)[0:1]
     first_slope = (1.0 - first_tanh * first_tanh).astype(jnp.bfloat16)
-    second_slope = (1.0 - second_tanh * second_tanh).astype(jnp.bfloat16)
+    second_slope = (weights * (1.0 - second_tanh * second_tanh)).astype(jnp.bfloat16)
     for k in range(count):
         at = pl.ds(pl.multiple_of((row + k) * hid, hid), hid)
         lanes = slice(k * side, (k + 1) * side)
@@ -387,7 +427,7 @@
     half, side = cot_s.shape
     groups = rows.shape[1] // side
     base = pl.multiple_of((place // slabs) * half, half)
-    unpack([near[n] for n in range(slabs)], place, place, film_s, rate_s, cot_s, class_s, base)
+    unpack([near[n] for n in range(slabs)], place, groups, film_s, rate_s, cot_s, class_s, base)
     mine = pl.ds(base, half)
     write_features(film_s[mine, :], rate_s[mine, :], feat_s)
     local_s[...] = feat_s[...].astype(jnp.bfloat16)
@@ -405,7 +445,7 @@
 def far_kernel(
     scale, far, first_cls, rows, lanes, conv_l, mixing, mix_t, flux_col,
     film_i, rate_i, back_i, featb_i, act1_i, act2_i, slope1_i, slope2_i, flux_i,
-    grads, source, source_grad, height_own, pre_first,
+    grads, source, source_grad, pre_first,
     film_s, rate_s, back_s, featb, act1_s, act2_s, slope1_s, slope2_s, flux_s,
     cot_s, class_s, feat_s, sgrad_s, pre_s,
 ):
@@ -417,7 +457,7 @@
     groups = rows.shape[1] // side
     upper = place // slabs
     base = pl.multiple_of((1 - upper) * half, half)
-    unpack([far[n] for n in range(slabs)], place ^ slabs, place, film_s, rate_s, cot_s, class_s, base)
+    unpack([far[n] for n in range(slabs)], place ^ slabs, groups, film_s, rate_s, cot_s, class_s, base)
     mine = pl.ds(base, half)
     back_s[mine, :] = masked_products(cot_s[...], rows[0], rows[1], class_s[...], groups)
     sgrad_s[...] = products_masked(lanes[2], lanes[3], back_s[...], first_cls[...], groups)
@@ -440,6 +480,7 @@
     pre_s[(side + 1) * hid :, :] = jnp.zeros((hid, side), jnp.bfloat16)
     mixing_sum = conv_sum = flux_sum = None
     chunk = FAR_CHUNK
+    ones = jnp.ones((4 * side, side), jnp.bfloat16)
     for start in range(0, side, chunk):
         def joined(ref):
             return jnp.concatenate([ref[(start + k) * hid : (start + k + 1) * hid, :] for k in range(chunk)], axis=1)
@@ -447,8 +488,8 @@
         flux_cot = time_step * jnp.concatenate(
             [sgrad_s[start + k : start + k + 1, :] for k in range(chunk)], axis=1
         )
-        second_cot = (weights * flux_cot).astype(jnp.bfloat16)
-        pre_second = second_cot * joined(slope2_s)
+        cot_rows = jnp.broadcast_to(flux_cot, (hid, chunk * side)).astype(jnp.bfloat16)
+        pre_second = cot_rows * joined(slope2_s)
         first_cot = dot(mixing[...], pre_second).astype(jnp.bfloat16)
         pre_cot = first_cot * joined(slope1_s)
         for k in range(chunk):
@@ -459,15 +500,17 @@
         )
         mixing_part = dot_lanes(joined(act1_s), pre_second)
         conv_part = dot_lanes(stacked, pre_cot)
-        product = joined(act2_s).astype(jnp.float32) * flux_cot
-        flux_part = sum(product[:, k * side : (k + 1) * side] for k in range(chunk))
+        product = joined(act2_s) * cot_rows
+        while product.shape[1] > 4 * side:
+            product = product[:, : product.shape[1] // 2] + product[:, product.shape[1] // 2 :]
+        flux_part = dot(product, ones)
         if start == 0:
             mixing_sum, conv_sum, flux_sum = mixing_part, conv_part, flux_part
         else:
             mixing_sum += mixing_part
             conv_sum += conv_part
             flux_sum += flux_part
-    flux_rows = jnp.broadcast_to(jnp.sum(flux_sum, axis=1, keepdims=True), (hid, 16)).T
+    flux_rows = flux_sum[:, :16].T
     side_by_side = jnp.concatenate(
         [mixing_sum, jnp.concatenate([conv_sum, flux_rows], axis=0)], axis=1
     )
@@ -476,7 +519,6 @@
     source[...] = film_s[...] + time_step * (flux_s[...] - maskf * jnp.abs(rate_s[...]))
     at = pl.multiple_of(place * own_rows, own_rows)
     source_grad[...] = sgrad_s[pl.ds(at, own_rows), :]
-    height_own[...] = film_s[pl.ds(at, own_rows), :]
     pre_first[...] = pre_s[pl.ds(pl.multiple_of(at * hid, hid), (own_rows + 2) * hid), :]
 
 
@@ -485,7 +527,7 @@
     final_film, film_grad, feature_s,
 ):
     place = lax.axis_index("sp")
-    own_rows, side = height.shape
+    own_rows, side = source_grad.shape
     groups = rows.shape[1] // side
     hid = taps_l.shape[1] // 3
     at = pl.multiple_of(place * own_rows, own_rows)
@@ -508,7 +550,7 @@
         after = jnp.where(lane == side - 1, 0.0, pltpu.roll(first, side - 1, 1))
         before = jnp.where(lane == 0, 0.0, pltpu.roll(last, 1, 1))
         cots.append((after + middle + before).astype(jnp.bfloat16).astype(jnp.float32))
-    film_grad[0] = source_grad[...] + cots[0] + 2.0 * height[...] * cots[1]
+    film_grad[0] = source_grad[...] + cots[0] + 2.0 * height[0] * cots[1]
 
 
 def finish_kernel(here, there, conv_grad, mixing_grad, flux_grad):
@@ -544,18 +586,27 @@
     params = pltpu.CompilerParams(vmem_limit_bytes=40 * 2**20)
     shape = jax.ShapeDtypeStruct
 
-    length = 3 * own_rows + 8
-
-    def placed(value, number):
-        at = number * own_rows
-        rows, lanes = value.shape[1:]
-        return jnp.pad(value, ((0, 0), (at, length - at - rows), (0, side - lanes)))
-
-    rate = placed(evaporation, 1)
-    near = jnp.where(placed(contact_mask, 1) != 0, -rate, rate)
-    near = near + placed(film_start, 0) + placed(film_cotangent, 2)
-    near = near + placed(second_classes.reshape(1, 1, own_rows), 3).astype(f32)
-    near = lax.optimization_barrier(near)
+    def in_hbm(*arrays):
+        return [pltpu.with_memory_space_constraint(array, pltpu.HBM) for array in arrays]
+
+    hbm = pl.BlockSpec(memory_space=pltpu.HBM)
+    near, height = pl.pallas_call(
+        partial(pack_kernel, groups),
+        out_shape=[shape((1, PLANES * own_rows, side), bf16), shape((1, own_rows, side), f32)],
+        in_specs=[hbm] * 5,
+        scratch_shapes=[
+            pltpu.VMEM((1, own_rows, side), f32),
+            pltpu.VMEM((1, own_rows, side), jnp.int32),
+            pltpu.VMEM((1, own_rows), jnp.int32),
+            pltpu.VMEM((1, own_rows, side), f32),
+            pltpu.SemaphoreType.DMA((5,)),
+        ],
+        compiler_params=params,
+    )(
+        *in_hbm(
+            film_start, evaporation, contact_mask, second_classes.reshape(1, own_rows), film_cotangent
+        )
+    )
     weights = (
         span_inverses,
         conv_weight,
@@ -575,7 +626,7 @@
             shape((hid, 1), f32),
             shape((1, side), jnp.int32),
         ],
-        in_specs=[pl.BlockSpec(memory_space=pltpu.HBM)] * len(weights),
+        in_specs=[hbm] * len(weights),
         scratch_shapes=[
             pltpu.VMEM(span_inverses.shape, f32),
             pltpu.VMEM(conv_weight.shape, bf16),
@@ -584,7 +635,7 @@
             pltpu.SemaphoreType.DMA((len(weights),)),
         ],
         compiler_params=params,
-    )(*(pltpu.with_memory_space_constraint(weight, pltpu.HBM) for weight in weights))
+    )(*in_hbm(*weights))
     far = None
     bit = 1
     while bit < sp:
@@ -620,17 +671,16 @@
         ],
         compiler_params=params,
     )(near, rows, conv_l, mix_t, flux_col)
-    grads, source, source_grad, height, pre_first, *_ = pl.pallas_call(
+    grads, source, source_grad, pre_first, *_ = pl.pallas_call(
         partial(far_kernel, scale),
         out_shape=[
             shape((hid, 2 * hid), f32),
             shape((side, side), f32),
             shape((own_rows, side), f32),
-            shape((own_rows, side), f32),
             shape(((own_rows + 2) * hid, side), bf16),
         ]
         + kept,
-        input_output_aliases={8 + number: 5 + number for number in range(len(kept))},
+        input_output_aliases={8 + number: 4 + number for number in range(len(kept))},
         scratch_shapes=[
             pltpu.VMEM((half, side), f32),
             pltpu.VMEM((half, side), f32),
@@ -666,18 +716,19 @@
 def on_device(film_start, *others):
     own_rows, side = film_start.shape[1:]
     nspan = others[2].shape[2]
-    conv_weight = others[5]
+    channels, hid = others[5].shape[2:]
     sp, rep = lax.axis_size("sp"), lax.axis_size("rep")
     small = (
         film_start.shape[0] == 1
         and nspan == 1
-        and side == 128
+        and side % 128 == 0
+        and side * side * hid <= VMEM_VALUES
         and own_rows % 16 == 0
+        and sp > 1
         and sp & (sp - 1) == 0
         and rep & (rep - 1) == 0
-        and sp > 1
-        and conv_weight.shape[2] == 4
-        and conv_weight.shape[3] == 64
+        and channels == 4
+        and hid == 64
     )
     return (by_replica if small else by_slabs)(film_start, *others)
 

time: 27.8 us -> 25.4 us (0.914)
  starting transfers between devices: 11.2 us -> 10 us
  other arithmetic: 0.78 us -> 0.01 us
  waiting for transfers between devices: 6.14 us -> 5.45 us
    ppermute x5, starting transfers between devices: 11.2 us -> 10 us  [swap(): return lax.ppermute(value, axis, [(i, i ^ bit) for i in range(size)])]
    pallas_call x0 -> x1, Pallas kernels: none -> 0.89 us  [by_replica(): pl.pallas_call(partial(pack_kernel, groups), out_shape=[shape((1, PLANES...]
    add x1 -> x0, other arithmetic: 0.77 us -> none  [by_replica(): near = near + placed(second_classes.reshape(1, 1, own_rows), 3).astype(f32)]
    ppermute x5, waiting for transfers between devices: 6.14 us -> 5.45 us  [swap(): return lax.ppermute(value, axis, [(i, i ^ bit) for i in range(size)])]
    pallas_call x1, Pallas kernels: 4.36 us -> 3.74 us  [by_replica(): pl.pallas_call(partial(far_kernel, scale), out_shape=[shape((hid, 2 * hid...]
  transfers between devices with their start and end apart: 5 -> 5, of which waited for: 5 -> 5; matrix products, arithmetic and copies ran while one was open for 0% -> 0% of each run, Pallas kernels for 13% -> 15%
where the time goes in v1:
time: 25.4 us; the launch traced here: 25.1 us
  starting transfers between devices  10 us (39%)
  Pallas kernels  8.97 us (35%)
  waiting for transfers between devices  5.45 us (21%)
  between operations  0.66 us (3%)
    ppermute x5, starting transfers between devices, swap(): return lax.ppermute(value, axis, [(i, i ^ bit) for i in range(size)])  10 us
    ppermute x5, waiting for transfers between devices, swap(): return lax.ppermute(value, axis, [(i, i ^ bit) for i in range(size)])  5.45 us
    pallas_call x1, Pallas kernels, by_replica(): pl.pallas_call(partial(far_kernel, scale), out_shape=[shape((hid, 2 * hid...  3.74 us
    pallas_call x1, Pallas kernels, by_replica(): pl.pallas_call(near_kernel, out_shape=kept + [shape((own_rows, side), f32...  1.35 us
    pallas_call x1, Pallas kernels, by_replica(): pl.pallas_call(prepare_kernel, out_shape=[shape((4, groups * side, side),...  1.19 us
    pallas_call x1, Pallas kernels, by_replica(): pl.pallas_call(field_kernel, out_shape=[shape(film_start.shape, f32), sha...  1.12 us
    pallas_call x1, Pallas kernels, by_replica(): pl.pallas_call(partial(pack_kernel, groups), out_shape=[shape((1, PLANES...  0.89 us
    pallas_call x1, Pallas kernels, by_replica(): pl.pallas_call(finish_kernel, out_shape=[shape(conv_weight.shape, f32), s...  0.68 us
  transfers between devices with their start and end apart: 5, of which 5 were waited for; matrix products, arithmetic and copies ran while one was open for 0% of the time, Pallas kernels for 15%

profile of v1, /device:TPU:0, one launch (start us, length us, event | category | flops | bytes accessed | tf_op | source)
XLA Modules:
  0.0 25.1 jit_solution(1848667940836924543)
XLA Ops:
  0.6 0.9 %shard_map.137 = (bf16[1,64,128]{2,1,0:T(8,128)(2,1)S(1)}, f32[1,16,128]{2,1,0:T(8,128)S(1)}) custom-call(f32[1,16,128]{2,1,0:T(8,128)} %film_h.1, f32[1,16,128]{2,1,0:T(8,128)} %rate_h.1, s32[1,16,128]{2,1,0:T(8,128)} %mask_h.1, s32[1,16]{1,0:T(1,128)} %bitcast.4, f32[1,16,128]{2,1,0:T(8,128)} %cot_h.1), custom_call_target="tpu_custom_call" | custom-call | tf_op jit(solution)/shard_map/pallas_call | solution.py:593
  1.5 3.0 %collective-permute-start = (bf16[1,64,128]{2,1,0:T(8,128)(2,1)S(1)}, bf16[1,64,128]{2,1,0:T(8,128)(2,1)S(1)}, u32[]{:S(2)}, u32[]{:S(2)}) collective-permute-start(bf16[1,64,128]{2,1,0:T(8,128)(2,1)S(1)} %get-tuple-element.43), channel_id=1, source_target_pairs={{0,1},{1,0},{2,3},{3,2},{4,5},{5,4},{6,7},{7,6},{8,9},{9,8},{10,11... | collective-permute-start | bytes 49160 | tf_op jit(solution)/shard_map/ppermute | solution.py:260
  4.5 1.2 %shard_map.138 = (bf16[4,512,128]{2,1,0:T(8,128)(2,1)S(1)}, bf16[4,128,512]{2,1,0:T(8,128)(2,1)S(1)}, bf16[64,48]{1,0:T(8,128)(2,1)S(1)}, bf16[16,192]{1,0:T(8,1...) custom-call(f32[4,128,128]{2,1,0:T(8,128)} %inv_h.1, ...), custom_call_target="tpu_custom_call" | custom-call | tf_op jit(solution)/shard_map/pallas_call | solution.py:617
  5.7 0.5 %collective-permute-done = bf16[1,64,128]{2,1,0:T(8,128)(2,1)S(1)} collective-permute-done((bf16[1,64,128]{2,1,0:T(8,128)(2,1)S(1)}, bf16[1,64,128]{2,1,0:T(8,128)(2,1)S(1)}, u32[]{:S(2)}, u32[]{:S(2)}) %collective-permute-start) | collective-permute-done | bytes 16416 | tf_op jit(solution)/shard_map/ppermute | solution.py:260
  6.3 2.1 %collective-permute-start.1 = (bf16[2,64,128]{2,1,0:T(8,128)(2,1)S(1)}, bf16[2,64,128]{2,1,0:T(8,128)(2,1)S(1)}, u32[]{:S(2)}, u32[]{:S(2)}) collective-permute-start(bf16[2,64,128]{2,1,0:T(8,128)(2,1)S(1)} %pad_maximum_fusion), channel_id=1, source_target_pairs={{0,2},{1,3},{2,0},{3,1},{4,6},{5,7},{6,4},{7,5},{8,10},{9,11},{10,... | collective-permute-start | bytes 98312 | tf_op jit(solution)/shard_map/ppermute | solution.py:260
  8.4 1.9 %collective-permute-done.1 = bf16[2,64,128]{2,1,0:T(8,128)(2,1)S(1)} collective-permute-done((bf16[2,64,128]{2,1,0:T(8,128)(2,1)S(1)}, bf16[2,64,128]{2,1,0:T(8,128)(2,1)S(1)}, u32[]{:S(2)}, u32[]{:S(2)}) %collective-permute-start.1) | collective-permute-done | bytes 32800 | tf_op jit(solution)/shard_map/ppermute | solution.py:260
  10.3 3.0 %collective-permute-start.2 = (bf16[4,64,128]{2,1,0:T(8,128)(2,1)S(1)}, bf16[4,64,128]{2,1,0:T(8,128)(2,1)S(1)}, u32[]{:S(2)}, u32[]{:S(2)}) collective-permute-start(bf16[4,64,128]{2,1,0:T(8,128)(2,1)S(1)} %constant_dynamic-update-slice_fusion.near), channel_id=1, source_target_pairs={{0,4},{1,5},{2,6},{3,7},{4,0},{5,1},{6,2},{7,3},{8,12},{9,13},{10,... | collective-permute-start | bytes 196616 | tf_op jit(solution)/shard_map/ppermute | solution.py:260
  13.3 1.4 %shard_map.139 = (f32[128,128]{1,0:T(8,128)S(1)}, f32[128,128]{1,0:T(8,128)S(1)}, f32[128,128]{1,0:T(8,128)S(1)}, bf16[2080,128]{1,0:T(8,128)(2,1)S(1)}, bf16[81...) custom-call(bf16[4,64,128]{2,1,0:T(8,128)(2,1)S(1)} %constant_dynami, ...), custom_call_target="tpu_custom_call" | custom-call | tf_op jit(solution)/shard_map/pallas_call | solution.py:663
  14.7 0.9 %collective-permute-done.2.far = bf16[4,64,128]{2,1,0:T(8,128)(2,1)S(1)} collective-permute-done((bf16[4,64,128]{2,1,0:T(8,128)(2,1)S(1)}, bf16[4,64,128]{2,1,0:T(8,128)(2,1)S(1)}, u32[]{:S(2)}, u32[]{:S(2)}) %collective-permute-start.2) | collective-permute-done | bytes 65568 | tf_op jit(solution)/shard_map/ppermute | solution.py:260
  15.5 3.7 %shard_map.140 = (f32[64,128]{1,0:T(8,128)S(1)}, f32[128,128]{1,0:T(8,128)S(1)}, f32[16,128]{1,0:T(8,128)S(1)}, bf16[1152,128]{1,0:T(8,128)(2,1)S(1)}, f32[128,1...) custom-call(bf16[4,64,128]{2,1,0:T(8,128)(2,1)S(1)} %collective-perm, ...), custom_call_target="tpu_custom_call", output_to_operand_aliasing={{4}: (8, {}), {5}: (9, {}), {6}: (10, {}), {7}: (11, {}), {... | custom-call | tf_op jit(solution)/shard_map/pallas_call | solution.py:674
  19.3 0.0 collective-permute-start.3
  19.3 1.2 %collective-permute-done.3 = f32[64,128]{1,0:T(8,128)S(1)} collective-permute-done((f32[64,128]{1,0:T(8,128)S(1)}, f32[64,128]{1,0:T(8,128)S(1)}, u32[]{:S(2)}, u32[]{:S(2)}) %collective-permute-start.3) | collective-permute-done | bytes 32800 | tf_op jit(solution)/shard_map/ppermute | solution.py:260
  20.5 1.9 %collective-permute-start.4 = (f32[64,128]{1,0:T(8,128)S(1)}, f32[64,128]{1,0:T(8,128)S(1)}, u32[]{:S(2)}, u32[]{:S(2)}) collective-permute-start(f32[64,128]{1,0:T(8,128)S(1)} %add.3.here), channel_id=1, source_target_pairs={{0,16},{8,24},{16,0},{24,8},{1,17},{9,25},{17,1},{25,9},{2,18},{10... | collective-permute-start | bytes 98312 | tf_op jit(solution)/shard_map/ppermute | solution.py:260
  22.4 1.1 %shard_map.141 = (f32[1,16,128]{2,1,0:T(8,128)}, f32[1,16,128]{2,1,0:T(8,128)}) custom-call(f32[128,128]{1,0:T(8,128)S(1)} %get-tuple-element.69.source, f32[16,128]{1,0:T(8,128)S(1)} %get-tuple-element.70.source_grad, f32[1,16,128]{2,1,0:T(8,128)S(1)} %get-tuple-element.71.height, bf16[1152,128]{1,0:T(8,128)(2,1)S(1)} %get-tuple-element.72.pre_first, ...), custom_call_target="tpu_custom_call" | custom-call | tf_op jit(solution)/shard_map/pallas_call | solution.py:694
  23.5 0.9 %collective-permute-done.4.there = f32[64,128]{1,0:T(8,128)S(1)} collective-permute-done((f32[64,128]{1,0:T(8,128)S(1)}, f32[64,128]{1,0:T(8,128)S(1)}, u32[]{:S(2)}, u32[]{:S(2)}) %collective-permute-start.4) | collective-permute-done | bytes 32800 | tf_op jit(solution)/shard_map/ppermute | solution.py:260
  24.4 0.7 %shard_map.142 = (f32[3,3,4,64]{3,2,1,0:T(4,128)}, f32[64,64]{1,0:T(8,128)}, f32[1,64]{1,0:T(1,128)}) custom-call(f32[64,128]{1,0:T(8,128)S(1)} %add.3.here, f32[64,128]{1,0:T(8,128)S(1)} %collective-permute-done.4.there), custom_call_target="tpu_custom_call" | custom-call | tf_op jit(solution)/shard_map/pallas_call | solution.py:708
  (4 shorter events, 0.0 us)
Async XLA Ops:
  1.5 4.7 %collective-permute-start = (bf16[1,64,128]{2,1,0:T(8,128)(2,1)S(1)}, bf16[1,64,128]{2,1,0:T(8,128)(2,1)S(1)}, u32[]{:S(2)}, u32[]{:S(2)}) collective-permute-start(bf16[1,64,128]{2,1,0:T(8,128)(2,1)S(1)} %get-tuple-element.43), channel_id=1, source_target_pairs={{0,1},{1,0},{2,3},{3,2},{4,5},{5,4},{6,7},{7,6},{8,9},{9,8},{10,11... | collective-permute-start | bytes 49160 | tf_op jit(solution)/shard_map/ppermute | solution.py:260
  6.3 4.0 %collective-permute-start.1 = (bf16[2,64,128]{2,1,0:T(8,128)(2,1)S(1)}, bf16[2,64,128]{2,1,0:T(8,128)(2,1)S(1)}, u32[]{:S(2)}, u32[]{:S(2)}) collective-permute-start(bf16[2,64,128]{2,1,0:T(8,128)(2,1)S(1)} %pad_maximum_fusion), channel_id=1, source_target_pairs={{0,2},{1,3},{2,0},{3,1},{4,6},{5,7},{6,4},{7,5},{8,10},{9,11},{10,... | collective-permute-start | bytes 98312 | tf_op jit(solution)/shard_map/ppermute | solution.py:260
  10.3 5.3 %collective-permute-start.2 = (bf16[4,64,128]{2,1,0:T(8,128)(2,1)S(1)}, bf16[4,64,128]{2,1,0:T(8,128)(2,1)S(1)}, u32[]{:S(2)}, u32[]{:S(2)}) collective-permute-start(bf16[4,64,128]{2,1,0:T(8,128)(2,1)S(1)} %constant_dynamic-update-slice_fusion.near), channel_id=1, source_target_pairs={{0,4},{1,5},{2,6},{3,7},{4,0},{5,1},{6,2},{7,3},{8,12},{9,13},{10,... | collective-permute-start | bytes 196616 | tf_op jit(solution)/shard_map/ppermute | solution.py:260
  19.3 1.2 %collective-permute-start.3 = (f32[64,128]{1,0:T(8,128)S(1)}, f32[64,128]{1,0:T(8,128)S(1)}, u32[]{:S(2)}, u32[]{:S(2)}) collective-permute-start(f32[64,128]{1,0:T(8,128)S(1)} %get-tuple-element.77), channel_id=1, source_target_pairs={{0,8},{8,0},{16,24},{24,16},{1,9},{9,1},{17,25},{25,17},{2,10},{10... | collective-permute-start | bytes 98312 | tf_op jit(solution)/shard_map/ppermute | solution.py:260
  20.5 3.9 %collective-permute-start.4 = (f32[64,128]{1,0:T(8,128)S(1)}, f32[64,128]{1,0:T(8,128)S(1)}, u32[]{:S(2)}, u32[]{:S(2)}) collective-permute-start(f32[64,128]{1,0:T(8,128)S(1)} %add.3.here), channel_id=1, source_target_pairs={{0,16},{8,24},{16,0},{24,8},{1,17},{9,25},{17,1},{25,9},{2,18},{10... | collective-permute-start | bytes 98312 | tf_op jit(solution)/shard_map/ppermute | solution.py:260

commit v2 on v1

--- a/solution.py
+++ b/solution.py
@@ -290,8 +290,7 @@
     ]
     for copy in copies:
         copy.start()
-    for copy in copies:
-        copy.wait()
+    copies[3].wait()
     rows, side = film.shape[1:]
     bits = class_bits(groups)
     classes = jnp.broadcast_to(class_s[...].astype(jnp.float32), (side, rows)).T.astype(jnp.int32)
@@ -299,6 +298,8 @@
     bit = jnp.zeros((rows, side), jnp.int32)
     for number in range(bits):
         bit = jnp.where(lane // (side // bits) == number, (classes >> number) & 1, bit)
+    for number in (0, 1, 2, 4):
+        copies[number].wait()
     high, low = halves(film[0])
     packed[0, :rows] = jnp.where(bit != 0, -high, high)
     rate = rate_s[0].astype(jnp.bfloat16)
@@ -485,11 +486,11 @@
         def joined(ref):
             return jnp.concatenate([ref[(start + k) * hid : (start + k + 1) * hid, :] for k in range(chunk)], axis=1)
 
-        flux_cot = time_step * jnp.concatenate(
-            [sgrad_s[start + k : start + k + 1, :] for k in range(chunk)], axis=1
-        )
-        cot_rows = jnp.broadcast_to(flux_cot, (hid, chunk * side)).astype(jnp.bfloat16)
-        pre_second = cot_rows * joined(slope2_s)
+        cots = [
+            jnp.concatenate([jnp.broadcast_to(time_step * sgrad_s[start + k : start + k + 1, :], (16, side)).astype(jnp.bfloat16)] * (hid // 16), axis=0)
+            for k in range(chunk)
+        ]
+        pre_second = jnp.concatenate([cots[k] * slope2_s[(start + k) * hid : (start + k + 1) * hid, :] for k in range(chunk)], axis=1)
         first_cot = dot(mixing[...], pre_second).astype(jnp.bfloat16)
         pre_cot = first_cot * joined(slope1_s)
         for k in range(chunk):
@@ -500,9 +501,9 @@
         )
         mixing_part = dot_lanes(joined(act1_s), pre_second)
         conv_part = dot_lanes(stacked, pre_cot)
-        product = joined(act2_s) * cot_rows
-        while product.shape[1] > 4 * side:
-            product = product[:, : product.shape[1] // 2] + product[:, product.shape[1] // 2 :]
+        products = [cots[k] * act2_s[(start + k) * hid : (start + k + 1) * hid, :] for k in range(chunk)]
+        products = [sum(products[k : k + 8][1:], products[k]) for k in range(0, chunk, 8)]
+        product = jnp.concatenate(products, axis=1)
         flux_part = dot(product, ones)
         if start == 0:
             mixing_sum, conv_sum, flux_sum = mixing_part, conv_part, flux_part
@@ -554,7 +555,7 @@
 
 
 def finish_kernel(here, there, conv_grad, mixing_grad, flux_grad):
-    total = here[...] + there[...]
+    total = here[...].astype(jnp.float32) + there[...].astype(jnp.float32)
     hid = mixing_grad.shape[0]
     channels = conv_grad.shape[2]
     mixing_grad[...] = total[:, :hid]
@@ -583,7 +584,7 @@
     groups = span_inverses.shape[0]
     hid = mixing_weight.shape[0]
     sp, rep = lax.axis_size("sp"), lax.axis_size("rep")
-    params = pltpu.CompilerParams(vmem_limit_bytes=40 * 2**20)
+    params = pltpu.CompilerParams(vmem_limit_bytes=24 * 2**20)
     shape = jax.ShapeDtypeStruct
 
     def in_hbm(*arrays):
@@ -698,12 +699,12 @@
         compiler_params=params,
     )(source, source_grad, height, pre_first, first_cls, second_cls, rows, lanes, taps_l)
 
-    there = jnp.zeros_like(grads)
+    there = grads
     bit = 1
     while bit < rep:
         if bit > 1:
-            grads = grads + there
-        there = swap(grads, "rep", bit)
+            grads = grads.astype(f32) + there.astype(f32)
+        there = swap(grads, "rep", 2 * bit - 1)
         bit *= 2
     conv_grad, mixing_grad, flux_grad = pl.pallas_call(
         finish_kernel,

time: 25.4 us -> 24.7 us (0.972)
  waiting for transfers between devices: 5.45 us -> 5.1 us
    ppermute x5, waiting for transfers between devices: 5.45 us -> 5.1 us  [swap(): return lax.ppermute(value, axis, [(i, i ^ bit) for i in range(size)])]
where the time goes in v2:
time: 24.7 us; the launch traced here: 24.4 us
  starting transfers between devices  9.77 us (40%)
  Pallas kernels  8.87 us (36%)
  waiting for transfers between devices  5.1 us (21%)
  between operations  0.66 us (3%)
    ppermute x5, starting transfers between devices, swap(): return lax.ppermute(value, axis, [(i, i ^ bit) for i in range(size)])  9.77 us
    ppermute x5, waiting for transfers between devices, swap(): return lax.ppermute(value, axis, [(i, i ^ bit) for i in range(size)])  5.1 us
    pallas_call x1, Pallas kernels, by_replica(): pl.pallas_call(partial(far_kernel, scale), out_shape=[shape((hid, 2 * hid...  3.68 us
    pallas_call x1, Pallas kernels, by_replica(): pl.pallas_call(near_kernel, out_shape=kept + [shape((own_rows, side), f32...  1.36 us
    pallas_call x1, Pallas kernels, by_replica(): pl.pallas_call(prepare_kernel, out_shape=[shape((4, groups * side, side),...  1.19 us
    pallas_call x1, Pallas kernels, by_replica(): pl.pallas_call(field_kernel, out_shape=[shape(film_start.shape, f32), sha...  1.12 us
    pallas_call x1, Pallas kernels, by_replica(): pl.pallas_call(partial(pack_kernel, groups), out_shape=[shape((1, PLANES...  0.84 us
    pallas_call x1, Pallas kernels, by_replica(): pl.pallas_call(finish_kernel, out_shape=[shape(conv_weight.shape, f32), s...  0.68 us
  transfers between devices with their start and end apart: 5, of which 5 were waited for; matrix products, arithmetic and copies ran while one was open for 0% of the time, Pallas kernels for 15%

profile of v2, /device:TPU:0, one launch (start us, length us, event | category | flops | bytes accessed | tf_op | source)
XLA Modules:
  0.0 24.4 jit_solution(16126724076412187498)
XLA Ops:
  0.6 0.8 %shard_map.137 = (bf16[1,64,128]{2,1,0:T(8,128)(2,1)S(1)}, f32[1,16,128]{2,1,0:T(8,128)S(1)}) custom-call(f32[1,16,128]{2,1,0:T(8,128)} %film_h.1, f32[1,16,128]{2,1,0:T(8,128)} %rate_h.1, s32[1,16,128]{2,1,0:T(8,128)} %mask_h.1, s32[1,16]{1,0:T(1,128)} %bitcast.4, f32[1,16,128]{2,1,0:T(8,128)} %cot_h.1), custom_call_target="tpu_custom_call" | custom-call | tf_op jit(solution)/shard_map/pallas_call | solution.py:594
  1.5 3.0 %collective-permute-start = (bf16[1,64,128]{2,1,0:T(8,128)(2,1)S(1)}, bf16[1,64,128]{2,1,0:T(8,128)(2,1)S(1)}, u32[]{:S(2)}, u32[]{:S(2)}) collective-permute-start(bf16[1,64,128]{2,1,0:T(8,128)(2,1)S(1)} %get-tuple-element.43), channel_id=1, source_target_pairs={{0,1},{1,0},{2,3},{3,2},{4,5},{5,4},{6,7},{7,6},{8,9},{9,8},{10,11... | collective-permute-start | bytes 49160 | tf_op jit(solution)/shard_map/ppermute | solution.py:260
  4.5 1.2 %shard_map.138 = (bf16[4,512,128]{2,1,0:T(8,128)(2,1)S(1)}, bf16[4,128,512]{2,1,0:T(8,128)(2,1)S(1)}, bf16[64,48]{1,0:T(8,128)(2,1)S(1)}, bf16[16,192]{1,0:T(8,1...) custom-call(f32[4,128,128]{2,1,0:T(8,128)} %inv_h.1, ...), custom_call_target="tpu_custom_call" | custom-call | tf_op jit(solution)/shard_map/pallas_call | solution.py:618
  5.7 0.5 %collective-permute-done = bf16[1,64,128]{2,1,0:T(8,128)(2,1)S(1)} collective-permute-done((bf16[1,64,128]{2,1,0:T(8,128)(2,1)S(1)}, bf16[1,64,128]{2,1,0:T(8,128)(2,1)S(1)}, u32[]{:S(2)}, u32[]{:S(2)}) %collective-permute-start) | collective-permute-done | bytes 16416 | tf_op jit(solution)/shard_map/ppermute | solution.py:260
  6.2 2.1 %collective-permute-start.1 = (bf16[2,64,128]{2,1,0:T(8,128)(2,1)S(1)}, bf16[2,64,128]{2,1,0:T(8,128)(2,1)S(1)}, u32[]{:S(2)}, u32[]{:S(2)}) collective-permute-start(bf16[2,64,128]{2,1,0:T(8,128)(2,1)S(1)} %pad_maximum_fusion), channel_id=1, source_target_pairs={{0,2},{1,3},{2,0},{3,1},{4,6},{5,7},{6,4},{7,5},{8,10},{9,11},{10,... | collective-permute-start | bytes 98312 | tf_op jit(solution)/shard_map/ppermute | solution.py:260
  8.3 1.9 %collective-permute-done.1 = bf16[2,64,128]{2,1,0:T(8,128)(2,1)S(1)} collective-permute-done((bf16[2,64,128]{2,1,0:T(8,128)(2,1)S(1)}, bf16[2,64,128]{2,1,0:T(8,128)(2,1)S(1)}, u32[]{:S(2)}, u32[]{:S(2)}) %collective-permute-start.1) | collective-permute-done | bytes 32800 | tf_op jit(solution)/shard_map/ppermute | solution.py:260
  10.2 3.0 %collective-permute-start.2 = (bf16[4,64,128]{2,1,0:T(8,128)(2,1)S(1)}, bf16[4,64,128]{2,1,0:T(8,128)(2,1)S(1)}, u32[]{:S(2)}, u32[]{:S(2)}) collective-permute-start(bf16[4,64,128]{2,1,0:T(8,128)(2,1)S(1)} %constant_dynamic-update-slice_fusion.near), channel_id=1, source_target_pairs={{0,4},{1,5},{2,6},{3,7},{4,0},{5,1},{6,2},{7,3},{8,12},{9,13},{10,... | collective-permute-start | bytes 196616 | tf_op jit(solution)/shard_map/ppermute | solution.py:260
  13.2 1.4 %shard_map.139 = (f32[128,128]{1,0:T(8,128)S(1)}, f32[128,128]{1,0:T(8,128)S(1)}, f32[128,128]{1,0:T(8,128)S(1)}, bf16[2080,128]{1,0:T(8,128)(2,1)S(1)}, bf16[81...) custom-call(bf16[4,64,128]{2,1,0:T(8,128)(2,1)S(1)} %constant_dynami, ...), custom_call_target="tpu_custom_call" | custom-call | tf_op jit(solution)/shard_map/pallas_call | solution.py:664
  14.6 0.9 %collective-permute-done.2.far = bf16[4,64,128]{2,1,0:T(8,128)(2,1)S(1)} collective-permute-done((bf16[4,64,128]{2,1,0:T(8,128)(2,1)S(1)}, bf16[4,64,128]{2,1,0:T(8,128)(2,1)S(1)}, u32[]{:S(2)}, u32[]{:S(2)}) %collective-permute-start.2) | collective-permute-done | bytes 65568 | tf_op jit(solution)/shard_map/ppermute | solution.py:260
  15.5 3.7 %shard_map.140 = (f32[64,128]{1,0:T(8,128)S(1)}, f32[128,128]{1,0:T(8,128)S(1)}, f32[16,128]{1,0:T(8,128)S(1)}, bf16[1152,128]{1,0:T(8,128)(2,1)S(1)}, f32[128,1...) custom-call(bf16[4,64,128]{2,1,0:T(8,128)(2,1)S(1)} %collective-perm, ...), custom_call_target="tpu_custom_call", output_to_operand_aliasing={{4}: (8, {}), {5}: (9, {}), {6}: (10, {}), {7}: (11, {}), {... | custom-call | tf_op jit(solution)/shard_map/pallas_call | solution.py:675
  19.2 0.0 collective-permute-start.3
  19.2 1.2 %collective-permute-done.3 = f32[64,128]{1,0:T(8,128)S(1)} collective-permute-done((f32[64,128]{1,0:T(8,128)S(1)}, f32[64,128]{1,0:T(8,128)S(1)}, u32[]{:S(2)}, u32[]{:S(2)}) %collective-permute-start.3) | collective-permute-done | bytes 32800 | tf_op jit(solution)/shard_map/ppermute | solution.py:260
  20.4 1.6 %collective-permute-start.4 = (f32[64,128]{1,0:T(8,128)S(1)}, f32[64,128]{1,0:T(8,128)S(1)}, u32[]{:S(2)}, u32[]{:S(2)}) collective-permute-start(f32[64,128]{1,0:T(8,128)S(1)} %add.3.here), channel_id=1, source_target_pairs={{0,24},{8,16},{16,8},{24,0},{1,25},{9,17},{17,9},{25,1},{2,26},{10... | collective-permute-start | bytes 98312 | tf_op jit(solution)/shard_map/ppermute | solution.py:260
  22.0 1.1 %shard_map.141 = (f32[1,16,128]{2,1,0:T(8,128)}, f32[1,16,128]{2,1,0:T(8,128)}) custom-call(f32[128,128]{1,0:T(8,128)S(1)} %get-tuple-element.69.source, f32[16,128]{1,0:T(8,128)S(1)} %get-tuple-element.70.source_grad, f32[1,16,128]{2,1,0:T(8,128)S(1)} %get-tuple-element.71.height, bf16[1152,128]{1,0:T(8,128)(2,1)S(1)} %get-tuple-element.72.pre_first, ...), custom_call_target="tpu_custom_call" | custom-call | tf_op jit(solution)/shard_map/pallas_call | solution.py:695
  23.1 0.6 %collective-permute-done.4.there = f32[64,128]{1,0:T(8,128)S(1)} collective-permute-done((f32[64,128]{1,0:T(8,128)S(1)}, f32[64,128]{1,0:T(8,128)S(1)}, u32[]{:S(2)}, u32[]{:S(2)}) %collective-permute-start.4) | collective-permute-done | bytes 32800 | tf_op jit(solution)/shard_map/ppermute | solution.py:260
  23.7 0.7 %shard_map.142 = (f32[3,3,4,64]{3,2,1,0:T(4,128)}, f32[64,64]{1,0:T(8,128)}, f32[1,64]{1,0:T(1,128)}) custom-call(f32[64,128]{1,0:T(8,128)S(1)} %add.3.here, f32[64,128]{1,0:T(8,128)S(1)} %collective-permute-done.4.there), custom_call_target="tpu_custom_call" | custom-call | tf_op jit(solution)/shard_map/pallas_call | solution.py:709
  (4 shorter events, 0.0 us)
Async XLA Ops:
  1.5 4.7 %collective-permute-start = (bf16[1,64,128]{2,1,0:T(8,128)(2,1)S(1)}, bf16[1,64,128]{2,1,0:T(8,128)(2,1)S(1)}, u32[]{:S(2)}, u32[]{:S(2)}) collective-permute-start(bf16[1,64,128]{2,1,0:T(8,128)(2,1)S(1)} %get-tuple-element.43), channel_id=1, source_target_pairs={{0,1},{1,0},{2,3},{3,2},{4,5},{5,4},{6,7},{7,6},{8,9},{9,8},{10,11... | collective-permute-start | bytes 49160 | tf_op jit(solution)/shard_map/ppermute | solution.py:260
  6.2 4.0 %collective-permute-start.1 = (bf16[2,64,128]{2,1,0:T(8,128)(2,1)S(1)}, bf16[2,64,128]{2,1,0:T(8,128)(2,1)S(1)}, u32[]{:S(2)}, u32[]{:S(2)}) collective-permute-start(bf16[2,64,128]{2,1,0:T(8,128)(2,1)S(1)} %pad_maximum_fusion), channel_id=1, source_target_pairs={{0,2},{1,3},{2,0},{3,1},{4,6},{5,7},{6,4},{7,5},{8,10},{9,11},{10,... | collective-permute-start | bytes 98312 | tf_op jit(solution)/shard_map/ppermute | solution.py:260
  10.2 5.3 %collective-permute-start.2 = (bf16[4,64,128]{2,1,0:T(8,128)(2,1)S(1)}, bf16[4,64,128]{2,1,0:T(8,128)(2,1)S(1)}, u32[]{:S(2)}, u32[]{:S(2)}) collective-permute-start(bf16[4,64,128]{2,1,0:T(8,128)(2,1)S(1)} %constant_dynamic-update-slice_fusion.near), channel_id=1, source_target_pairs={{0,4},{1,5},{2,6},{3,7},{4,0},{5,1},{6,2},{7,3},{8,12},{9,13},{10,... | collective-permute-start | bytes 196616 | tf_op jit(solution)/shard_map/ppermute | solution.py:260
  19.2 1.2 %collective-permute-start.3 = (f32[64,128]{1,0:T(8,128)S(1)}, f32[64,128]{1,0:T(8,128)S(1)}, u32[]{:S(2)}, u32[]{:S(2)}) collective-permute-start(f32[64,128]{1,0:T(8,128)S(1)} %get-tuple-element.77), channel_id=1, source_target_pairs={{0,8},{8,0},{16,24},{24,16},{1,9},{9,1},{17,25},{25,17},{2,10},{10... | collective-permute-start | bytes 98312 | tf_op jit(solution)/shard_map/ppermute | solution.py:260
  20.4 3.3 %collective-permute-start.4 = (f32[64,128]{1,0:T(8,128)S(1)}, f32[64,128]{1,0:T(8,128)S(1)}, u32[]{:S(2)}, u32[]{:S(2)}) collective-permute-start(f32[64,128]{1,0:T(8,128)S(1)} %add.3.here), channel_id=1, source_target_pairs={{0,24},{8,16},{16,8},{24,0},{1,25},{9,17},{17,9},{25,1},{2,26},{10... | collective-permute-start | bytes 98312 | tf_op jit(solution)/shard_map/ppermute | solution.py:260

commit v3 on v2

--- a/solution.py
+++ b/solution.py
@@ -348,9 +348,11 @@
     flux_col[...] = wide.T[:, :1]
 
 
-def masked_products(left, rows_high, rows_low, classes, groups):
+def masked_products(left, rows_high, rows_low, classes, groups, short=False):
     high, low = halves(left)
     high = jnp.concatenate([jnp.where(classes == g, high, 0) for g in range(groups)], axis=1)
+    if short:
+        return dot(high, rows_high) + dot(high, rows_low)
     low = jnp.concatenate([jnp.where(classes == g, low, 0) for g in range(groups)], axis=1)
     return dot(high, rows_high) + dot(low, rows_high) + dot(high, rows_low)
 
@@ -440,7 +442,7 @@
             local_s, start, base + start, NEAR_CHUNK, conv_l, mix_t, weights,
             act1_s, act2_s, slope1_s, slope2_s, flux_s,
         )
-    back_s[mine, :] = masked_products(cot_s[...], rows[0], rows[1], class_s[...], groups)
+    back_s[mine, :] = masked_products(cot_s[...], rows[0], rows[1], class_s[...], groups, True)
 
 
 def far_kernel(
@@ -460,7 +462,7 @@
     base = pl.multiple_of((1 - upper) * half, half)
     unpack([far[n] for n in range(slabs)], place ^ slabs, groups, film_s, rate_s, cot_s, class_s, base)
     mine = pl.ds(base, half)
-    back_s[mine, :] = masked_products(cot_s[...], rows[0], rows[1], class_s[...], groups)
+    back_s[mine, :] = masked_products(cot_s[...], rows[0], rows[1], class_s[...], groups, True)
     sgrad_s[...] = products_masked(lanes[2], lanes[3], back_s[...], first_cls[...], groups)
     write_features(film_s[mine, :], rate_s[mine, :], feat_s)
     featb[pl.ds(pl.multiple_of((base + 1) * 16, 16), half * 16), :] = feat_s[
@@ -481,7 +483,7 @@
     pre_s[(side + 1) * hid :, :] = jnp.zeros((hid, side), jnp.bfloat16)
     mixing_sum = conv_sum = flux_sum = None
     chunk = FAR_CHUNK
-    ones = jnp.ones((4 * side, side), jnp.bfloat16)
+    ones = jnp.ones((16, 4 * side), jnp.bfloat16)
     for start in range(0, side, chunk):
         def joined(ref):
             return jnp.concatenate([ref[(start + k) * hid : (start + k + 1) * hid, :] for k in range(chunk)], axis=1)
@@ -504,14 +506,14 @@
         products = [cots[k] * act2_s[(start + k) * hid : (start + k + 1) * hid, :] for k in range(chunk)]
         products = [sum(products[k : k + 8][1:], products[k]) for k in range(0, chunk, 8)]
         product = jnp.concatenate(products, axis=1)
-        flux_part = dot(product, ones)
+        flux_part = dot_lanes(product, ones)
         if start == 0:
             mixing_sum, conv_sum, flux_sum = mixing_part, conv_part, flux_part
         else:
             mixing_sum += mixing_part
             conv_sum += conv_part
             flux_sum += flux_part
-    flux_rows = flux_sum[:, :16].T
+    flux_rows = flux_sum.T
     side_by_side = jnp.concatenate(
         [mixing_sum, jnp.concatenate([conv_sum, flux_rows], axis=0)], axis=1
     )

time: 24.7 us -> 24.6 us (level)
  no operation moved by 1% of the time
where the time goes in v3:
time: 24.6 us; the launch traced here: 24.4 us
  starting transfers between devices  9.8 us (40%)
  Pallas kernels  8.8 us (36%)
  waiting for transfers between devices  5.08 us (21%)
  between operations  0.66 us (3%)
    ppermute x5, starting transfers between devices, swap(): return lax.ppermute(value, axis, [(i, i ^ bit) for i in range(size)])  9.8 us
    ppermute x5, waiting for transfers between devices, swap(): return lax.ppermute(value, axis, [(i, i ^ bit) for i in range(size)])  5.08 us
    pallas_call x1, Pallas kernels, by_replica(): pl.pallas_call(partial(far_kernel, scale), out_shape=[shape((hid, 2 * hid...  3.63 us
    pallas_call x1, Pallas kernels, by_replica(): pl.pallas_call(near_kernel, out_shape=kept + [shape((own_rows, side), f32...  1.35 us
    pallas_call x1, Pallas kernels, by_replica(): pl.pallas_call(prepare_kernel, out_shape=[shape((4, groups * side, side),...  1.19 us
    pallas_call x1, Pallas kernels, by_replica(): pl.pallas_call(field_kernel, out_shape=[shape(film_start.shape, f32), sha...  1.12 us
    pallas_call x1, Pallas kernels, by_replica(): pl.pallas_call(partial(pack_kernel, groups), out_shape=[shape((1, PLANES...  0.84 us
    pallas_call x1, Pallas kernels, by_replica(): pl.pallas_call(finish_kernel, out_shape=[shape(conv_weight.shape, f32), s...  0.68 us
  transfers between devices with their start and end apart: 5, of which 5 were waited for; matrix products, arithmetic and copies ran while one was open for 0% of the time, Pallas kernels for 15%

profile of v3, /device:TPU:0, one launch (start us, length us, event | category | flops | bytes accessed | tf_op | source)
XLA Modules:
  0.0 24.4 jit_solution(12052975000362574554)
XLA Ops:
  0.6 0.8 %shard_map.137 = (bf16[1,64,128]{2,1,0:T(8,128)(2,1)S(1)}, f32[1,16,128]{2,1,0:T(8,128)S(1)}) custom-call(f32[1,16,128]{2,1,0:T(8,128)} %film_h.1, f32[1,16,128]{2,1,0:T(8,128)} %rate_h.1, s32[1,16,128]{2,1,0:T(8,128)} %mask_h.1, s32[1,16]{1,0:T(1,128)} %bitcast.4, f32[1,16,128]{2,1,0:T(8,128)} %cot_h.1), custom_call_target="tpu_custom_call" | custom-call | tf_op jit(solution)/shard_map/pallas_call | solution.py:596
  1.5 3.0 %collective-permute-start = (bf16[1,64,128]{2,1,0:T(8,128)(2,1)S(1)}, bf16[1,64,128]{2,1,0:T(8,128)(2,1)S(1)}, u32[]{:S(2)}, u32[]{:S(2)}) collective-permute-start(bf16[1,64,128]{2,1,0:T(8,128)(2,1)S(1)} %get-tuple-element.43), channel_id=1, source_target_pairs={{0,1},{1,0},{2,3},{3,2},{4,5},{5,4},{6,7},{7,6},{8,9},{9,8},{10,11... | collective-permute-start | bytes 49160 | tf_op jit(solution)/shard_map/ppermute | solution.py:260
  4.5 1.2 %shard_map.138 = (bf16[4,512,128]{2,1,0:T(8,128)(2,1)S(1)}, bf16[4,128,512]{2,1,0:T(8,128)(2,1)S(1)}, bf16[64,48]{1,0:T(8,128)(2,1)S(1)}, bf16[16,192]{1,0:T(8,1...) custom-call(f32[4,128,128]{2,1,0:T(8,128)} %inv_h.1, ...), custom_call_target="tpu_custom_call" | custom-call | tf_op jit(solution)/shard_map/pallas_call | solution.py:620
  5.7 0.5 %collective-permute-done = bf16[1,64,128]{2,1,0:T(8,128)(2,1)S(1)} collective-permute-done((bf16[1,64,128]{2,1,0:T(8,128)(2,1)S(1)}, bf16[1,64,128]{2,1,0:T(8,128)(2,1)S(1)}, u32[]{:S(2)}, u32[]{:S(2)}) %collective-permute-start) | collective-permute-done | bytes 16416 | tf_op jit(solution)/shard_map/ppermute | solution.py:260
  6.2 2.1 %collective-permute-start.1 = (bf16[2,64,128]{2,1,0:T(8,128)(2,1)S(1)}, bf16[2,64,128]{2,1,0:T(8,128)(2,1)S(1)}, u32[]{:S(2)}, u32[]{:S(2)}) collective-permute-start(bf16[2,64,128]{2,1,0:T(8,128)(2,1)S(1)} %pad_maximum_fusion), channel_id=1, source_target_pairs={{0,2},{1,3},{2,0},{3,1},{4,6},{5,7},{6,4},{7,5},{8,10},{9,11},{10,... | collective-permute-start | bytes 98312 | tf_op jit(solution)/shard_map/ppermute | solution.py:260
  8.3 1.9 %collective-permute-done.1 = bf16[2,64,128]{2,1,0:T(8,128)(2,1)S(1)} collective-permute-done((bf16[2,64,128]{2,1,0:T(8,128)(2,1)S(1)}, bf16[2,64,128]{2,1,0:T(8,128)(2,1)S(1)}, u32[]{:S(2)}, u32[]{:S(2)}) %collective-permute-start.1) | collective-permute-done | bytes 32800 | tf_op jit(solution)/shard_map/ppermute | solution.py:260
  10.2 3.0 %collective-permute-start.2 = (bf16[4,64,128]{2,1,0:T(8,128)(2,1)S(1)}, bf16[4,64,128]{2,1,0:T(8,128)(2,1)S(1)}, u32[]{:S(2)}, u32[]{:S(2)}) collective-permute-start(bf16[4,64,128]{2,1,0:T(8,128)(2,1)S(1)} %constant_dynamic-update-slice_fusion.near), channel_id=1, source_target_pairs={{0,4},{1,5},{2,6},{3,7},{4,0},{5,1},{6,2},{7,3},{8,12},{9,13},{10,... | collective-permute-start | bytes 196616 | tf_op jit(solution)/shard_map/ppermute | solution.py:260
  13.2 1.3 %shard_map.139 = (f32[128,128]{1,0:T(8,128)S(1)}, f32[128,128]{1,0:T(8,128)S(1)}, f32[128,128]{1,0:T(8,128)S(1)}, bf16[2080,128]{1,0:T(8,128)(2,1)S(1)}, bf16[81...) custom-call(bf16[4,64,128]{2,1,0:T(8,128)(2,1)S(1)} %constant_dynami, ...), custom_call_target="tpu_custom_call" | custom-call | tf_op jit(solution)/shard_map/pallas_call | solution.py:666
  14.6 0.9 %collective-permute-done.2.far = bf16[4,64,128]{2,1,0:T(8,128)(2,1)S(1)} collective-permute-done((bf16[4,64,128]{2,1,0:T(8,128)(2,1)S(1)}, bf16[4,64,128]{2,1,0:T(8,128)(2,1)S(1)}, u32[]{:S(2)}, u32[]{:S(2)}) %collective-permute-start.2) | collective-permute-done | bytes 65568 | tf_op jit(solution)/shard_map/ppermute | solution.py:260
  15.5 3.6 %shard_map.140 = (f32[64,128]{1,0:T(8,128)S(1)}, f32[128,128]{1,0:T(8,128)S(1)}, f32[16,128]{1,0:T(8,128)S(1)}, bf16[1152,128]{1,0:T(8,128)(2,1)S(1)}, f32[128,1...) custom-call(bf16[4,64,128]{2,1,0:T(8,128)(2,1)S(1)} %collective-perm, ...), custom_call_target="tpu_custom_call", output_to_operand_aliasing={{4}: (8, {}), {5}: (9, {}), {6}: (10, {}), {7}: (11, {}), {... | custom-call | tf_op jit(solution)/shard_map/pallas_call | solution.py:677
  19.1 0.0 collective-permute-start.3
  19.1 1.2 %collective-permute-done.3 = f32[64,128]{1,0:T(8,128)S(1)} collective-permute-done((f32[64,128]{1,0:T(8,128)S(1)}, f32[64,128]{1,0:T(8,128)S(1)}, u32[]{:S(2)}, u32[]{:S(2)}) %collective-permute-start.3) | collective-permute-done | bytes 32800 | tf_op jit(solution)/shard_map/ppermute | solution.py:260
  20.3 1.7 %collective-permute-start.4 = (f32[64,128]{1,0:T(8,128)S(1)}, f32[64,128]{1,0:T(8,128)S(1)}, u32[]{:S(2)}, u32[]{:S(2)}) collective-permute-start(f32[64,128]{1,0:T(8,128)S(1)} %add.3.here), channel_id=1, source_target_pairs={{0,24},{8,16},{16,8},{24,0},{1,25},{9,17},{17,9},{25,1},{2,26},{10... | collective-permute-start | bytes 98312 | tf_op jit(solution)/shard_map/ppermute | solution.py:260
  22.0 1.1 %shard_map.141 = (f32[1,16,128]{2,1,0:T(8,128)}, f32[1,16,128]{2,1,0:T(8,128)}) custom-call(f32[128,128]{1,0:T(8,128)S(1)} %get-tuple-element.69.source, f32[16,128]{1,0:T(8,128)S(1)} %get-tuple-element.70.source_grad, f32[1,16,128]{2,1,0:T(8,128)S(1)} %get-tuple-element.71.height, bf16[1152,128]{1,0:T(8,128)(2,1)S(1)} %get-tuple-element.72.pre_first, ...), custom_call_target="tpu_custom_call" | custom-call | tf_op jit(solution)/shard_map/pallas_call | solution.py:697
  23.1 0.6 %collective-permute-done.4.there = f32[64,128]{1,0:T(8,128)S(1)} collective-permute-done((f32[64,128]{1,0:T(8,128)S(1)}, f32[64,128]{1,0:T(8,128)S(1)}, u32[]{:S(2)}, u32[]{:S(2)}) %collective-permute-start.4) | collective-permute-done | bytes 32800 | tf_op jit(solution)/shard_map/ppermute | solution.py:260
  23.7 0.7 %shard_map.142 = (f32[3,3,4,64]{3,2,1,0:T(4,128)}, f32[64,64]{1,0:T(8,128)}, f32[1,64]{1,0:T(1,128)}) custom-call(f32[64,128]{1,0:T(8,128)S(1)} %add.3.here, f32[64,128]{1,0:T(8,128)S(1)} %collective-permute-done.4.there), custom_call_target="tpu_custom_call" | custom-call | tf_op jit(solution)/shard_map/pallas_call | solution.py:711
  (4 shorter events, 0.0 us)
Async XLA Ops:
  1.5 4.7 %collective-permute-start = (bf16[1,64,128]{2,1,0:T(8,128)(2,1)S(1)}, bf16[1,64,128]{2,1,0:T(8,128)(2,1)S(1)}, u32[]{:S(2)}, u32[]{:S(2)}) collective-permute-start(bf16[1,64,128]{2,1,0:T(8,128)(2,1)S(1)} %get-tuple-element.43), channel_id=1, source_target_pairs={{0,1},{1,0},{2,3},{3,2},{4,5},{5,4},{6,7},{7,6},{8,9},{9,8},{10,11... | collective-permute-start | bytes 49160 | tf_op jit(solution)/shard_map/ppermute | solution.py:260
  6.2 4.0 %collective-permute-start.1 = (bf16[2,64,128]{2,1,0:T(8,128)(2,1)S(1)}, bf16[2,64,128]{2,1,0:T(8,128)(2,1)S(1)}, u32[]{:S(2)}, u32[]{:S(2)}) collective-permute-start(bf16[2,64,128]{2,1,0:T(8,128)(2,1)S(1)} %pad_maximum_fusion), channel_id=1, source_target_pairs={{0,2},{1,3},{2,0},{3,1},{4,6},{5,7},{6,4},{7,5},{8,10},{9,11},{10,... | collective-permute-start | bytes 98312 | tf_op jit(solution)/shard_map/ppermute | solution.py:260
  10.2 5.3 %collective-permute-start.2 = (bf16[4,64,128]{2,1,0:T(8,128)(2,1)S(1)}, bf16[4,64,128]{2,1,0:T(8,128)(2,1)S(1)}, u32[]{:S(2)}, u32[]{:S(2)}) collective-permute-start(bf16[4,64,128]{2,1,0:T(8,128)(2,1)S(1)} %constant_dynamic-update-slice_fusion.near), channel_id=1, source_target_pairs={{0,4},{1,5},{2,6},{3,7},{4,0},{5,1},{6,2},{7,3},{8,12},{9,13},{10,... | collective-permute-start | bytes 196616 | tf_op jit(solution)/shard_map/ppermute | solution.py:260
  19.1 1.2 %collective-permute-start.3 = (f32[64,128]{1,0:T(8,128)S(1)}, f32[64,128]{1,0:T(8,128)S(1)}, u32[]{:S(2)}, u32[]{:S(2)}) collective-permute-start(f32[64,128]{1,0:T(8,128)S(1)} %get-tuple-element.77), channel_id=1, source_target_pairs={{0,8},{8,0},{16,24},{24,16},{1,9},{9,1},{17,25},{25,17},{2,10},{10... | collective-permute-start | bytes 98312 | tf_op jit(solution)/shard_map/ppermute | solution.py:260
  20.3 3.3 %collective-permute-start.4 = (f32[64,128]{1,0:T(8,128)S(1)}, f32[64,128]{1,0:T(8,128)S(1)}, u32[]{:S(2)}, u32[]{:S(2)}) collective-permute-start(f32[64,128]{1,0:T(8,128)S(1)} %add.3.here), channel_id=1, source_target_pairs={{0,24},{8,16},{16,8},{24,0},{1,25},{9,17},{17,9},{25,1},{2,26},{10... | collective-permute-start | bytes 98312 | tf_op jit(solution)/shard_map/ppermute | solution.py:260
